TPU v7x, 512 devices: a whole 4x4x16 slice. The times are simulated.
512 devices in a mesh: ctx: 8 (over z_hi, core), grp: 64 (over y, x, z_lo).
Axes of the slice: x: 4, y: 4, z: 16 (z_hi: 4, z_lo: 4; z = z_hi * 4 + z_lo), core: 2. Of those that a mesh axis runs over, the one named last changes fastest.
Arguments:
- queries: bfloat16 [128, 4096, 576], P('grp', 'ctx'), may hold values from -32 to 32
- kv_latent: bfloat16 [4096, 576], P(('ctx', 'grp')), may hold values from -8 to 8
- vert_tiles: int32 [64, 6], replicated, may hold values from 0 to 31
- slash_offsets: int32 [64, 4], replicated, may hold values from 1 to 31
- w_uv: bfloat16 [128, 512, 128], P('grp'), may hold values from -0.25 to 0.25
Outputs:
- attended: bfloat16 [128, 4096, 128], P('grp', 'ctx')
All inputs are finite; a program needn't handle non-finite values.
Results may differ from a plain program's by a relative error of at most 0.0055.
Values may be sent and summed in bfloat16 or wider, within the bound.
No kernel may reach another device: no remote copies, remote signals or barrier semaphores. Data moves between devices by JAX's collectives and lax.ppermute only.
A program may use at most 64 MiB of HBM per device.

v0:
```python
import jax
import jax.numpy as jnp
from jax import lax
from jax.sharding import PartitionSpec as P

TILE = 128
AMAX = 11
MIG = 1


score_scale = 192.0 ** (-0.5)
masked_score = -1e30


def swapped(array, axis, apart):
    return lax.ppermute(array, axis, [(i, i ^ 1 << apart) for i in range(lax.axis_size(axis))])


def active_tiles(vert_row, slash_row, block_index, tile_count):
    columns = jnp.arange(tile_count, dtype=jnp.int32)
    on_vert = jnp.any(columns[:, None] == vert_row[None, :], axis=1)
    on_slash = jnp.any((block_index - columns)[:, None] == slash_row[None, :], axis=1)
    return (columns <= block_index) & ((columns == block_index) | on_vert | on_slash)


def pair_loads(own_vert, own_slash, other_vert, other_slash, own_ids, tile_count):
    own_table = jax.vmap(
        lambda block_index: active_tiles(own_vert, own_slash, block_index, tile_count)
    )(own_ids)
    other_table = jax.vmap(
        lambda block_index: active_tiles(other_vert, other_slash, block_index, tile_count)
    )(own_ids)
    load_self = jnp.sum(own_table.astype(jnp.int32))
    load_other = jnp.sum(other_table.astype(jnp.int32))
    return (load_self > load_other, load_other > load_self)


def with_guest(
    queries, guest_queries, own_ids, own_vert, own_slash, other_vert, other_slash, giving, taking
):
    block_count = own_ids.shape[0]
    query_all = jnp.concatenate([queries, guest_queries], axis=1)
    block_ids = jnp.concatenate([own_ids, own_ids[block_count - MIG :]])
    vert_rows = jnp.concatenate(
        [jnp.broadcast_to(own_vert[None, :], (block_count, own_vert.shape[0])), other_vert[None, :]]
    )
    slash_rows = jnp.concatenate(
        [
            jnp.broadcast_to(own_slash[None, :], (block_count, own_slash.shape[0])),
            other_slash[None, :],
        ]
    )
    kept = (jnp.arange(block_count, dtype=jnp.int32) < block_count - MIG) | jnp.logical_not(giving)
    live = jnp.concatenate([kept, jnp.broadcast_to(taking, (MIG,))])
    return (query_all, block_ids, vert_rows, slash_rows, live)


def on_device(queries, kv_latent, vert_tiles, slash_offsets, w_uv):
    head_count, row_count, kv_width = queries.shape
    latent_width = w_uv.shape[1]
    block_count = row_count // TILE
    tile_count = block_count * lax.axis_size("ctx")
    ctx_at = lax.axis_index("ctx")
    grp_at = lax.axis_index("grp")
    own_ids = ctx_at * block_count + jnp.arange(block_count, dtype=jnp.int32)
    own_vert = vert_tiles[grp_at]
    own_slash = slash_offsets[grp_at]
    keep_rows = (block_count - MIG) * TILE
    partner = jnp.bitwise_xor(grp_at, 1)
    other_vert = vert_tiles[partner]
    other_slash = slash_offsets[partner]
    giving, taking = pair_loads(own_vert, own_slash, other_vert, other_slash, own_ids, tile_count)
    guest_queries = swapped(queries[:, keep_rows:], "grp", 0)
    query_all, block_ids, vert_rows, slash_rows, live = with_guest(
        queries,
        guest_queries,
        own_ids,
        own_vert,
        own_slash,
        other_vert,
        other_slash,
        giving,
        taking,
    )
    block_total = block_ids.shape[0]
    live_table = (
        jax.vmap(
            lambda vert_row, slash_row, block_index: active_tiles(
                vert_row, slash_row, block_index, tile_count
            )
        )(vert_rows, slash_rows, block_ids)
        & live[:, None]
    )
    initial = (
        jnp.full((head_count, block_total * TILE), masked_score, jnp.float32),
        jnp.zeros((head_count, block_total * TILE), jnp.float32),
        jnp.zeros((head_count, block_total * TILE, latent_width), jnp.float32),
    )
    whole_latent = lax.all_gather(kv_latent, ("ctx", "grp"), axis=0, tiled=True)
    arrived_count = whole_latent.shape[0] // TILE
    arrived_tiles = whole_latent.reshape(arrived_count, TILE, kv_width)
    first_tile = jnp.int32(0) // TILE
    tile_cap = min(arrived_count, AMAX)
    group_tiles = max(1, min(tile_cap, 512 // TILE))
    turn_most = -(-tile_cap // group_tiles)

    def one_block(block_index, state_now):
        tile_live = live_table[block_index]
        live_count = jnp.sum(tile_live.astype(jnp.int32))
        picked = jnp.nonzero(tile_live, size=turn_most * group_tiles, fill_value=0)[0].astype(
            jnp.int32
        )
        turn_count = (live_count + group_tiles - 1) // group_tiles
        query_block = lax.dynamic_slice_in_dim(query_all, block_index * TILE, TILE, 1)
        query_pos = block_ids[block_index] * TILE + jnp.arange(TILE, dtype=jnp.int32)

        def one_turn(turn_index, inner_state):
            top_all, total_all, accum_all = inner_state
            chosen = lax.dynamic_slice_in_dim(picked, turn_index * group_tiles, group_tiles)
            slot_live = (
                turn_index * group_tiles + jnp.arange(group_tiles, dtype=jnp.int32) < live_count
            )
            key_rows = arrived_tiles[chosen].reshape(group_tiles * TILE, kv_width)
            key_pos = (
                (first_tile + chosen)[:, None] * TILE + jnp.arange(TILE, dtype=jnp.int32)[None, :]
            ).reshape(-1)
            allowed = jnp.repeat(slot_live, TILE)[None, :] & (
                key_pos[None, :] <= query_pos[:, None]
            )
            scores = (
                jnp.einsum("hqc,kc->hqk", query_block, key_rows, preferred_element_type=jnp.float32)
                * score_scale
            )
            scores = jnp.where(allowed[None], scores, masked_score)
            top_old = lax.dynamic_slice_in_dim(top_all, block_index * TILE, TILE, 1)
            total_old = lax.dynamic_slice_in_dim(total_all, block_index * TILE, TILE, 1)
            accum_old = lax.dynamic_slice_in_dim(accum_all, block_index * TILE, TILE, 1)
            top_new = jnp.maximum(top_old, jnp.max(scores, axis=2))
            weights = jnp.where(allowed[None], jnp.exp(scores - top_new[:, :, None]), 0.0)
            rescale = jnp.exp(top_old - top_new)
            total_new = rescale * total_old + jnp.sum(weights, axis=2)
            accum_new = rescale[:, :, None] * accum_old + jnp.einsum(
                "hqk,kc->hqc",
                weights.astype(jnp.bfloat16),
                key_rows[:, :latent_width],
                preferred_element_type=jnp.float32,
            )
            top_all = lax.dynamic_update_slice_in_dim(top_all, top_new, block_index * TILE, 1)
            total_all = lax.dynamic_update_slice_in_dim(total_all, total_new, block_index * TILE, 1)
            accum_all = lax.dynamic_update_slice_in_dim(accum_all, accum_new, block_index * TILE, 1)
            return (top_all, total_all, accum_all)

        return lax.fori_loop(0, turn_count, one_turn, state_now)

    running = lax.fori_loop(0, block_total, one_block, initial)
    top_all, total_all, accum_all = running
    safe_total = jnp.where(total_all > 0.0, total_all, 1.0)
    latent = (accum_all / safe_total[:, :, None]).astype(jnp.bfloat16)
    own_up = jnp.einsum(
        "hqc,hcd->hqd", latent[:, :row_count], w_uv, preferred_element_type=jnp.float32
    ).astype(jnp.bfloat16)
    returned = swapped(latent[:, row_count:], "grp", 0)
    tail_rows = jnp.einsum(
        "hqc,hcd->hqd", returned, w_uv, preferred_element_type=jnp.float32
    ).astype(jnp.bfloat16)
    final_tail = jnp.where(giving, tail_rows, own_up[:, keep_rows:])
    return jnp.concatenate([own_up[:, :keep_rows], final_tail], axis=1)


def solution(mesh):
    placed = (P("grp", "ctx", None), P(("ctx", "grp"), None), P(), P(), P("grp", None, None))
    return jax.shard_map(
        on_device, mesh=mesh, in_specs=placed, out_specs=P("grp", "ctx", None), check_vma=False
    )
```

profile of v0, /device:TPU:483, one launch (start us, length us, event | category | flops | bytes accessed | tf_op | source)
XLA Modules:
  0.0 1544.3 jit_solution(11077368857709601967)
XLA Ops:
  6.5 0.7 all-gather.2.cloned.1.call-update
  7.3 1.0 slice.24
  8.2 2.6 collective-permute-start
  11.5 1.0 fusion.38
  12.5 1.0 fusion.37
  13.7 0.8 convert_reduce_fusion.1
  17.2 0.7 pad_add_fusion.3
  18.4 1.4 pad_maximum_fusion
  19.8 1384.7 %all-gather.2.cloned.1.call-done = bf16[4096,576]{1,0:T(8,128)(2,1)} async-done(((bf16[8,576]{1,0:T(8,128)(2,1)}), bf16[4096,576]{1,0:T(8,128)(2,1)}) %all-gather.2.cloned.1.call-update) | async-done | bytes 4718608 | tf_op jit(solution)/shard_map/all_gather | solution.py:99
  1404.5 1.8 broadcast_in_dim.132
  1406.3 121.0 %while.61 = (s32[]{:T(128)}, f32[2,640]{1,0:T(2,128)S(1)}, f32[2,640]{1,0:T(2,128)S(1)}, f32[2,640,512]{2,1,0:T(8,128)}, pred[5,32]{1,0:T(8,128)(4,1)S(1)}, /*in...) while((s32[]{:T(128)}, f32[2,640]{1,0:T(2,128)S(1)}, ...), condition=%wide.region_17.18_spmd, body=%wide.region_8.17_spmd.sunk | while | flops 286789280 | bytes 6110900 | solution.py:155
  1406.3 0.7 fusion.56
  1409.2 0.8 scatter_custom_fusion.5
  1410.2 0.6 compare_select_fusion.7
  1410.8 14.1 while.62
  1410.9 0.6 add_compare_fusion.2
  1411.9 3.2 gather_fusion
  1415.7 2.2 fusion.64
  1419.0 3.2 gather_fusion
  1422.7 2.2 fusion.64
  1424.9 0.7 fusion.56
  1427.8 0.8 scatter_custom_fusion.5
  1428.8 0.6 compare_select_fusion.7
  1429.4 21.1 %while.62 = (s32[]{:T(128)}, f32[2,640]{1,0:T(2,128)S(1)}, f32[2,640]{1,0:T(2,128)S(1)}, f32[2,640,512]{2,1,0:T(8,128)}, s32[]{:T(128)}, /*index=5*/s32[]{:T(128...) while((s32[]{:T(128)}, f32[2,640]{1,0:T(2,128)S(1)}, ...), condition=%wide.region_16.16_spmd.clone, body=%wide.region_13.15_spmd.clone.sunk | while | flops 286787744 | bytes 5519163 | solution.py:153
  1430.5 3.2 gather_fusion
  1434.3 2.2 fusion.64
  1437.6 3.2 gather_fusion
  1441.3 2.2 fusion.64
  1444.6 3.2 gather_fusion
  1448.3 2.2 fusion.64
  1450.6 0.7 fusion.56
  1453.4 0.8 scatter_custom_fusion.5
  1454.4 0.6 compare_select_fusion.7
  1455.1 21.1 %while.62 = (s32[]{:T(128)}, f32[2,640]{1,0:T(2,128)S(1)}, f32[2,640]{1,0:T(2,128)S(1)}, f32[2,640,512]{2,1,0:T(8,128)}, s32[]{:T(128)}, /*index=5*/s32[]{:T(128...) while((s32[]{:T(128)}, f32[2,640]{1,0:T(2,128)S(1)}, ...), condition=%wide.region_16.16_spmd.clone, body=%wide.region_13.15_spmd.clone.sunk | while | flops 286787744 | bytes 5519163 | solution.py:153
  1456.2 3.2 gather_fusion
  1459.9 2.2 fusion.64
  1463.2 3.2 gather_fusion
  1466.9 2.2 fusion.64
  1470.2 3.2 gather_fusion
  1473.9 2.2 fusion.64
  1476.1 0.7 fusion.56
  1479.0 0.8 scatter_custom_fusion.5
  1480.0 0.6 compare_select_fusion.7
  1480.6 21.1 %while.62 = (s32[]{:T(128)}, f32[2,640]{1,0:T(2,128)S(1)}, f32[2,640]{1,0:T(2,128)S(1)}, f32[2,640,512]{2,1,0:T(8,128)}, s32[]{:T(128)}, /*index=5*/s32[]{:T(128...) while((s32[]{:T(128)}, f32[2,640]{1,0:T(2,128)S(1)}, ...), condition=%wide.region_16.16_spmd.clone, body=%wide.region_13.15_spmd.clone.sunk | while | flops 286787744 | bytes 5519163 | solution.py:153
  1481.7 3.2 gather_fusion
  1485.5 2.2 fusion.64
  1488.8 3.2 gather_fusion
  1492.5 2.2 fusion.64
  1495.8 3.2 gather_fusion
  1499.5 2.2 fusion.64
  1501.7 0.7 fusion.56
  1504.6 0.8 scatter_custom_fusion.5
  1505.5 0.6 compare_select_fusion.7
  1506.2 21.1 %while.62 = (s32[]{:T(128)}, f32[2,640]{1,0:T(2,128)S(1)}, f32[2,640]{1,0:T(2,128)S(1)}, f32[2,640,512]{2,1,0:T(8,128)}, s32[]{:T(128)}, /*index=5*/s32[]{:T(128...) while((s32[]{:T(128)}, f32[2,640]{1,0:T(2,128)S(1)}, ...), condition=%wide.region_16.16_spmd.clone, body=%wide.region_13.15_spmd.clone.sunk | while | flops 286787744 | bytes 5519163 | solution.py:153
  1507.3 3.2 gather_fusion
  1511.0 2.2 fusion.64
  1514.4 3.2 gather_fusion
  1518.1 2.2 fusion.64
  1521.4 3.2 gather_fusion
  1525.1 2.2 fusion.64
  1527.4 2.0 divide_convert_fusion
  1529.4 1.9 collective-permute-start.1
  1531.8 4.7 collective-permute-done.1
  1536.7 0.7 pad_maximum_fusion.1
  (249 shorter events, 29.6 us)
Async XLA Ops:
  6.5 1524.8 %copy-start = (bf16[2,512,128]{2,1,0:T(8,128)(2,1)S(1)}, bf16[2,512,128]{2,1,0:T(8,128)(2,1)}, u32[]{:S(2)}) copy-start(bf16[2,512,128]{2,1,0:T(8,128)(2,1)} %param.13) | copy-start | bytes 786436
  6.5 1398.0 %all-gather.2.cloned.1.call-start = ((), (), s32[]{:S(2)}) async-start(), calls=%async_computation | async-start | bytes 5253120 | tf_op jit(solution)/shard_map/all_gather | solution.py:99
  8.2 10.2 collective-permute-start
  1529.4 7.1 collective-permute-start.1
Sparse Core Ops, SparseCore 0:
  9.6 1394.8 all-gather.1
where the time goes:
time: 1550 us; the launch traced here: 1540 us
  waiting for transfers between devices  1390 us (90%)
  local copies, waits for them, and re-layouts  54.5 us (4%)
  matrix products  37.3 us (2%)
  other arithmetic  34.6 us (2%)
  between operations  16 us (1%)
    all_gather x1, waiting for transfers between devices, on_device(): whole_latent = lax.all_gather(kv_latent, ('ctx', 'grp'), axis=0, tiled=True)  1380 us
    gather x14, local copies, waits for them, and re-layouts, one_turn(): key_rows = arrived_tiles[chosen].reshape(group_tiles * TILE, kv_width)  44.1 us
    dot_general x14, matrix products, one_turn(): jnp.einsum('hqk,kc->hqc', weights.astype(jnp.bfloat16), key_rows[:, :late...  31.2 us
  transfers between devices with their start and end apart: 3, of which 2 were waited for; matrix products, arithmetic and copies ran while one was open for 1% of the time, Pallas kernels for 0%

commit v1 on v0

v1 whole, which is shorter than its diff:
```python
import jax
import jax.numpy as jnp
from jax import lax
from jax.experimental import pallas as pl
from jax.experimental.pallas import tpu as pltpu
from jax.sharding import Mesh, PartitionSpec as P

TILE = 128
HEADS = 2
LAT = 512
KV = 576
ROWS = 512
BLOCKS = 4
SLOTS = 12
ROW_SCALE = 192.0 ** -0.5
DEAD = -1e30


def attend(vert, slash, place, q_ref, kv_ref, w_ref, out_ref, list_ref, s_ref):
    first = place[0] * BLOCKS
    row = lax.broadcasted_iota(jnp.int32, (HEADS * TILE, 2 * TILE), 0) & (TILE - 1)
    col = lax.broadcasted_iota(jnp.int32, (HEADS * TILE, 2 * TILE), 1)

    def keys(tile):
        zh = tile >> 3
        core = (tile >> 2) & 1
        y = tile & 3
        return kv_ref[core, y, :, zh].reshape(TILE, KV)

    for b in range(BLOCKS):
        i = first + b
        live = jnp.int32(0)
        for n in range(6):
            v = vert[n]
            live = live | jnp.where(v < i, jnp.int32(1) << v, 0)
        for n in range(4):
            v = i - slash[n]
            live = live | jnp.where(v >= 0, jnp.int32(1) << jnp.maximum(v, 0), 0)
        for n in range(1, SLOTS):
            list_ref[b, n] = i
        list_ref[b, 0] = i
        count = jnp.int32(1)
        for j in range(31):
            list_ref[b, count] = j
            count = count + ((live >> j) & 1)
        for n in range(SLOTS - 1, SLOTS):
            pass
        q = q_ref[:, b * TILE : (b + 1) * TILE, :].reshape(HEADS * TILE, KV)
        top = None
        for p in range(SLOTS // 2):
            k = jnp.concatenate([keys(list_ref[b, 2 * p]), keys(list_ref[b, 2 * p + 1])], axis=0)
            s = lax.dot_general(q, k, (((1,), (1,)), ((), ())), preferred_element_type=jnp.float32)
            s = s * ROW_SCALE
            if p == 0:
                ok = ((col < TILE) & (col <= row)) | ((col >= TILE) & (count > 1))
            else:
                ok = col < (count - 2 * p) * TILE
            s = jnp.where(ok, s, DEAD)
            s_ref[:, p * 2 * TILE : (p + 1) * 2 * TILE] = s
            t = jnp.max(s, axis=1, keepdims=True)
            top = t if top is None else jnp.maximum(top, t)
        total = jnp.zeros((HEADS * TILE, 1), jnp.float32)
        acc = jnp.zeros((HEADS * TILE, LAT), jnp.float32)
        for p in range(SLOTS // 2):
            v = jnp.concatenate([keys(list_ref[b, 2 * p]), keys(list_ref[b, 2 * p + 1])], axis=0)[:, :LAT]
            w = jnp.exp(s_ref[:, p * 2 * TILE : (p + 1) * 2 * TILE] - top)
            total = total + jnp.sum(w, axis=1, keepdims=True)
            acc = acc + jnp.dot(w.astype(jnp.bfloat16), v, preferred_element_type=jnp.float32)
        latent = (acc / total).astype(jnp.bfloat16)
        for h in range(HEADS):
            up = jnp.dot(latent[h * TILE : (h + 1) * TILE], w_ref[h], preferred_element_type=jnp.float32)
            out_ref[h, b * TILE : (b + 1) * TILE, :] = up.astype(jnp.bfloat16)


def attention(vert, slash, place, q, kv, w):
    smem = pl.BlockSpec(memory_space=pltpu.SMEM)
    vmem = pl.BlockSpec(memory_space=pltpu.VMEM)
    return pl.pallas_call(
        attend,
        out_shape=jax.ShapeDtypeStruct((HEADS, ROWS, 128), jnp.bfloat16),
        in_specs=[smem, smem, smem, vmem, vmem, vmem],
        out_specs=vmem,
        scratch_shapes=[
            pltpu.SMEM((BLOCKS, 32), jnp.int32),
            pltpu.VMEM((HEADS * TILE, SLOTS * TILE), jnp.float32),
        ],
        compiler_params=pltpu.CompilerParams(vmem_limit_bytes=40 * 1024 * 1024),
        name="attention",
    )(vert, slash, place, q, kv, w)


def on_device(queries, kv_latent, vert_tiles, slash_offsets, w_uv):
    spread = jnp.broadcast_to(kv_latent[None], (16, 8, KV))
    along = lax.all_to_all(spread, ("zh", "zl"), 0, 0)
    spread = jnp.broadcast_to(along.reshape(1, 128, KV), (16, 128, KV))
    plane = lax.all_to_all(spread, ("y", "x"), 0, 0)
    whole = lax.all_gather(plane, "core", axis=0)
    whole = whole.reshape(2, 4, 4, 4, 32, KV)
    ctx_at = lax.axis_index("zh") * 2 + lax.axis_index("core")
    grp_at = (lax.axis_index("y") * 4 + lax.axis_index("x")) * 4 + lax.axis_index("zl")
    place = jnp.reshape(ctx_at, (1,)).astype(jnp.int32)
    return attention(vert_tiles[grp_at], slash_offsets[grp_at], place, queries, whole, w_uv)


def solution(mesh):
    fine = Mesh(mesh.devices.reshape(4, 2, 4, 4, 4), ("zh", "core", "y", "x", "zl"))
    ctx, grp = ("zh", "core"), ("y", "x", "zl")
    placed = (P(grp, ctx, None), P(ctx + grp, None), P(), P(), P(grp, None, None))
    return jax.shard_map(
        on_device, mesh=fine, in_specs=placed, out_specs=P(grp, ctx, None), check_vma=False
    )
```

time: 1550 us -> 119 us (0.08)
  the two profiles are of different devices: /device:TPU:483 before, /device:TPU:1 now
where the time goes in v1:
time: 119 us; the launch traced here: 118 us
  blocking collectives  61 us (51%)
  waiting for transfers between devices  22.8 us (19%)
  local copies, waits for them, and re-layouts  13.4 us (11%)
  between operations  13.4 us (11%)
  Pallas kernels  7.53 us (6%)
    all_to_all x1, blocking collectives, on_device(): plane = lax.all_to_all(spread, ('y', 'x'), 0, 0)  33.2 us
    all_to_all x1, blocking collectives, on_device(): along = lax.all_to_all(spread, ('zh', 'zl'), 0, 0)  27.8 us
    all_gather x1, waiting for transfers between devices, on_device(): whole = lax.all_gather(plane, 'core', axis=0)  22.8 us
    all_gather x1, local copies, waits for them, and re-layouts, on_device(): whole = lax.all_gather(plane, 'core', axis=0)  7.64 us
    pallas_call x1, Pallas kernels, attention(): pl.pallas_call(attend, out_shape=jax.ShapeDtypeStruct((HEADS, ROWS, 128),...  7.53 us
    unnamed x11, local copies, waits for them, and re-layouts  4.08 us
  transfers between devices with their start and end apart: 1, of which 1 were waited for; matrix products, arithmetic and copies ran while one was open for 1% of the time, Pallas kernels for 0%

profile of v1, /device:TPU:1, one launch (start us, length us, event | category | flops | bytes accessed | tf_op | source)
XLA Modules:
  0.0 118.2 jit_solution(1191130771983203047)
XLA Ops:
  6.5 0.0 copy-start
  6.5 0.0 all-gather.3.cloned.1.call-start
  6.5 0.7 broadcast_in_dim.6
  7.3 27.8 %all_to_all.10 = bf16[16,8,576]{2,1,0:T(8,128)(2,1)S(1)} all-to-all(bf16[16,8,576]{2,1,0:T(8,128)(2,1)S(1)} %broadcast_in_dim.6), channel_id=1, replica_groups=mesh['zh'=4,'core'=2,'y'=4,'x'=4,'zl'=4] {'zh','zl'}, dimensions={0} | all-to-all | bytes 294912 | tf_op jit(solution)/shard_map/all_to_all | solution.py:94
  35.0 0.1 copy.10
  35.2 0.5 broadcast_in_dim.15
  35.6 33.2 %all_to_all.11 = bf16[16,128,576]{1,2,0:T(8,128)(2,1)} all-to-all(bf16[16,128,576]{1,2,0:T(8,128)(2,1)S(1)} %broadcast_in_dim.15), channel_id=1, replica_groups=mesh['zh'=4,'core'=2,'y'=4,'x'=4,'zl'=4] {'y','x'}, dimensions={0} | all-to-all | bytes 4718592 | tf_op jit(solution)/shard_map/all_to_all | solution.py:96
  68.8 0.0 copy-start.4
  68.8 0.0 copy-start.3
  68.8 0.0 all-gather.3.cloned.1.call-update
  68.9 0.0 copy-done
  68.9 0.2 dynamic-slice_reduce_fusion.vert
  69.1 0.4 copy-done.4
  69.5 0.2 dynamic-slice_reduce_fusion.1.slash
  69.7 0.4 copy-done.3
  70.1 0.7 copy.12.q_ref
  70.9 0.0 copy-start.2
  70.9 22.8 %all-gather.3.cloned.1.call-done = bf16[32,128,576]{1,2,0:T(8,128)(2,1)} async-done(((bf16[16,128,576]{1,2,0:T(8,128)(2,1)}), bf16[32,128,576]{1,2,0:T(8,128)(2,1)}) %all-gather.3.cloned.1.call-update) | async-done | bytes 4718608 | tf_op jit(solution)/shard_map/all_gather | solution.py:97
  93.7 7.6 %copy.11 = bf16[32,128,576]{2,1,0:T(8,128)(2,1)} copy(bf16[32,128,576]{1,2,0:T(8,128)(2,1)} %all-gather.3.cloned.1.call-done) | data formatting | bytes 9437184 | tf_op jit(solution)/shard_map/all_gather | solution.py:97
  101.3 0.0 copy-done.2
  101.3 0.0 copy-start.1
  101.3 2.5 %copy-done.1 = bf16[32,128,576]{2,1,0:T(8,128)(2,1)S(1)} copy-done((bf16[32,128,576]{2,1,0:T(8,128)(2,1)S(1)}, bf16[32,128,576]{2,1,0:T(8,128)(2,1)}, u32[]{:S(2)}) %copy-start.1) | copy-done | bytes 4718616
  103.8 7.5 %attention.1 = bf16[2,512,128]{2,1,0:T(8,128)(2,1)} custom-call(s32[6]{0:T(128)S(1)} %dynamic-slice_reduce_fusion.vert, s32[4]{0:T(128)S(1)} %dynamic-slice_reduce_fusion.1.slash, s32[1]{0:T(128)} %bitcast.place, bf16[2,512,576]{2,1,0:T(8,128)(2,1)S(1)} %copy.12.q_ref, bf16[2,4,4,4,32,576]{5,4,3,2,1,0:T(8,128)(2,1)S(1)} %bitcast.3, ...), custom_call_target="tpu_custom_call" | custom-call | tf_op jit(solution)/shard_map/attention/pallas_call | solution.py:78
Async XLA Ops:
  6.5 62.4 %copy-start = (s32[64,6]{0,1:T(8,128)S(1)}, s32[64,6]{0,1:T(8,128)}, u32[]{:S(2)}) copy-start(s32[64,6]{0,1:T(8,128)} %param.7) | copy-start | bytes 4612
  6.5 87.1 %all-gather.3.cloned.1.call-start = ((), (), s32[]{:S(2)}) async-start(), calls=%async_computation.2 | async-start | bytes 7077888 | tf_op jit(solution)/shard_map/all_gather | solution.py:97
  68.8 0.7 copy-start.4
  68.8 1.3 %copy-start.3 = (bf16[2,512,576]{1,2,0:T(8,128)(2,1)S(1)}, bf16[2,512,576]{1,2,0:T(8,128)(2,1)}, u32[]{:S(2)}) copy-start(bf16[2,512,576]{1,2,0:T(8,128)(2,1)} %param.5) | copy-start | bytes 3538948
  70.9 30.4 %copy-start.2 = (bf16[2,512,128]{2,1,0:T(8,128)(2,1)S(1)}, bf16[2,512,128]{2,1,0:T(8,128)(2,1)}, u32[]{:S(2)}) copy-start(bf16[2,512,128]{2,1,0:T(8,128)(2,1)} %w_ref.1) | copy-start | bytes 786436
  101.3 2.5 %copy-start.1 = (bf16[32,128,576]{2,1,0:T(8,128)(2,1)S(1)}, bf16[32,128,576]{2,1,0:T(8,128)(2,1)}, u32[]{:S(2)}) copy-start(bf16[32,128,576]{2,1,0:T(8,128)(2,1)} %copy.11) | copy-start | bytes 14155780
Sparse Core Ops, SparseCore 0:
  69.0 24.6 all-gather.2

commit v2 on v1

v2 whole, which is shorter than its diff:
```python
import functools

import jax
import jax.numpy as jnp
from jax import lax
from jax.experimental import pallas as pl
from jax.experimental.pallas import tpu as pltpu
from jax.sharding import Mesh, PartitionSpec as P

TILE = 128
HEADS = 2
LAT = 512
KV = 576
WIDE = 640
ROWS = 512
BLOCKS = 4
ROW_SCALE = 192.0 ** -0.5
DEAD = -1e30
ALL = ("zh", "core", "y", "x", "zl")


def attend(slots, place, vert, slash, q_ref, kv_ref, w_ref, out_ref, list_ref, s_ref):
    first = place[0] * BLOCKS
    core = place[1]
    row = lax.broadcasted_iota(jnp.int32, (HEADS * TILE, 2 * TILE), 0) & (TILE - 1)
    col = lax.broadcasted_iota(jnp.int32, (HEADS * TILE, 2 * TILE), 1)

    def keys(tile, width):
        zh, half, y = tile >> 3, (tile >> 2) & 1, tile & 3
        side = half ^ core
        start = jnp.where(half == 0, 4 * y, y)
        step = jnp.where(half == 0, 1, 4)
        return [kv_ref[side, start + step * n, zh, :, :width] for n in range(4)]

    def pair(b, p, width):
        return jnp.concatenate(keys(list_ref[b, 2 * p], width) + keys(list_ref[b, 2 * p + 1], width), axis=0)

    for b in range(BLOCKS):
        i = first + b
        live = jnp.int32(0)
        for n in range(6):
            v = vert[n]
            live = live | jnp.where(v < i, jnp.int32(1) << v, 0)
        for n in range(4):
            v = i - slash[n]
            live = live | jnp.where(v >= 0, jnp.int32(1) << jnp.maximum(v, 0), 0)
        for n in range(slots):
            list_ref[b, n] = i
        count = jnp.int32(1)
        for j in range(min(31, slots * 4)):
            bit = (live >> j) & 1
            list_ref[b, count] = jnp.where(bit == 1, j, i)
            count = count + bit
        q = q_ref[:, b * TILE : (b + 1) * TILE, :].reshape(HEADS * TILE, KV)
        top = None
        for p in range(slots // 2):
            s = lax.dot_general(q, pair(b, p, KV), (((1,), (1,)), ((), ())), preferred_element_type=jnp.float32)
            s = s * ROW_SCALE
            if p == 0:
                ok = ((col < TILE) & (col <= row)) | ((col >= TILE) & (count > 1))
            else:
                ok = col < (count - 2 * p) * TILE
            s = jnp.where(ok, s, DEAD)
            s_ref[:, p * 2 * TILE : (p + 1) * 2 * TILE] = s
            t = jnp.max(s, axis=1, keepdims=True)
            top = t if top is None else jnp.maximum(top, t)
        total = jnp.zeros((HEADS * TILE, 1), jnp.float32)
        acc = jnp.zeros((HEADS * TILE, LAT), jnp.float32)
        for p in range(slots // 2):
            w = jnp.exp(s_ref[:, p * 2 * TILE : (p + 1) * 2 * TILE] - top)
            total = total + jnp.sum(w, axis=1, keepdims=True)
            acc = acc + jnp.dot(w.astype(jnp.bfloat16), pair(b, p, LAT), preferred_element_type=jnp.float32)
        latent = (acc / total).astype(jnp.bfloat16)
        for h in range(HEADS):
            up = jnp.dot(latent[h * TILE : (h + 1) * TILE], w_ref[h], preferred_element_type=jnp.float32)
            out_ref[h, b * TILE : (b + 1) * TILE, :] = up.astype(jnp.bfloat16)


def attention(place, vert, slash, q, kv, w):
    slots = min(12, 8 * kv.shape[2])
    smem = pl.BlockSpec(memory_space=pltpu.SMEM)
    vmem = pl.BlockSpec(memory_space=pltpu.VMEM)
    return pl.pallas_call(
        functools.partial(attend, slots),
        out_shape=jax.ShapeDtypeStruct((HEADS, ROWS, 128), jnp.bfloat16),
        in_specs=[smem, smem, smem, vmem, vmem, vmem],
        out_specs=vmem,
        scratch_shapes=[
            pltpu.SMEM((BLOCKS, 32), jnp.int32),
            pltpu.VMEM((HEADS * TILE, slots * TILE), jnp.float32),
        ],
        compiler_params=pltpu.CompilerParams(vmem_limit_bytes=40 * 1024 * 1024),
        name="attention",
    )(place, vert, slash, q, kv, w)


def device_at(zh, core, y, x, zl):
    return (((zh * 2 + core) * 4 + y) * 4 + x) * 4 + zl


def lines(swapped):
    out = []
    for zh in range(4):
        for core in range(2):
            for at in range(4):
                for zl in range(4):
                    along_x = (core == 0) != swapped
                    out.append([device_at(zh, core, *((at, n) if along_x else (n, at)), zl) for n in range(4)])
    return out


def to_all(block, groups):
    return lax.all_to_all(jnp.broadcast_to(block[None], (4, *block.shape)), ALL, 0, 0, axis_index_groups=groups)


other_core = [(device_at(a, c, 0, 0, 0) + n, device_at(a, 1 - c, 0, 0, 0) + n) for a in range(4) for c in range(2) for n in range(64)]


def on_device(queries, kv_latent, vert_tiles, slash_offsets, w_uv):
    zh, core = lax.axis_index("zh"), lax.axis_index("core")
    grp_at = (lax.axis_index("y") * 4 + lax.axis_index("x")) * 4 + lax.axis_index("zl")
    place = jnp.stack([zh * 2 + core, core]).astype(jnp.int32)
    vert, slash = vert_tiles[grp_at], slash_offsets[grp_at]
    rows = jnp.pad(kv_latent, ((0, 0), (0, WIDE - KV)))
    column = lax.all_to_all(jnp.broadcast_to(rows[None], (16, 8, WIDE)), ("zh", "zl"), 0, 0)

    def plane(depth, column):
        block = column[: 4 * depth].reshape(depth, 32, WIDE)
        block = to_all(block, lines(False))
        own = to_all(block, lines(True))
        other = lax.ppermute(own, ALL, other_core)
        kv = jnp.stack([own, other]).reshape(2, 16, depth, 32, WIDE)
        return attention(place, vert, slash, queries, kv, w_uv)

    return lax.switch(zh, [functools.partial(plane, depth) for depth in range(1, 5)], column)


def solution(mesh):
    fine = Mesh(mesh.devices.reshape(4, 2, 4, 4, 4), ALL)
    ctx, grp = ("zh", "core"), ("y", "x", "zl")
    placed = (P(grp, ctx, None), P(ctx + grp, None), P(), P(), P(grp, None, None))
    return jax.shard_map(
        on_device, mesh=fine, in_specs=placed, out_specs=P(grp, ctx, None), check_vma=False
    )
```

time: 119 us -> 81.3 us (0.68)
  the two profiles are of different devices: /device:TPU:1 before, /device:TPU:481 now
where the time goes in v2:
time: 81.3 us; the launch traced here: 81 us
  blocking collectives  34.1 us (42%)
  starting transfers between devices  16.9 us (21%)
  waiting for transfers between devices  16.3 us (20%)
  Pallas kernels  6.76 us (8%)
  local copies, waits for them, and re-layouts  3.41 us (4%)
  other arithmetic  3.19 us (4%)
    all_to_all x2, blocking collectives, to_all(): lax.all_to_all(jnp.broadcast_to(block[None], (4, *block.shape)), ALL, 0,...  34.1 us
    all_to_all x1, waiting for transfers between devices, on_device(): lax.all_to_all(jnp.broadcast_to(rows[None], (16, 8, WIDE)), ('zh', 'zl'),...  12.4 us
    ppermute x1, starting transfers between devices, plane(): other = lax.ppermute(own, ALL, other_core)  8.61 us
    all_to_all x1, starting transfers between devices, on_device(): lax.all_to_all(jnp.broadcast_to(rows[None], (16, 8, WIDE)), ('zh', 'zl'),...  8.29 us
    pallas_call x1, Pallas kernels, attention(): pl.pallas_call(functools.partial(attend, slots), out_shape=jax.ShapeDtype...  6.76 us
    ppermute x1, waiting for transfers between devices, plane(): other = lax.ppermute(own, ALL, other_core)  3.89 us
    another operation x1, other arithmetic, plane(): kv = jnp.stack([own, other]).reshape(2, 16, depth, 32, WIDE)  3.11 us
  transfers between devices with their start and end apart: 2, of which 2 were waited for; matrix products, arithmetic and copies ran while one was open for 1% of the time, Pallas kernels for 0%

profile of v2, /device:TPU:481, one launch (start us, length us, event | category | flops | bytes accessed | tf_op | source)
XLA Modules:
  0.0 81.0 jit_solution(7470486756560015180)
XLA Ops:
  0.0 0.7 pad.4
  0.7 0.7 broadcast_in_dim.49
  1.4 8.3 %all-to-all-start.8 = ((bf16[16,8,640]{2,1,0:T(8,128)(2,1)}), bf16[16,8,640]{2,1,0:T(8,128)(2,1)S(1)}, u32[]{:S(2)}, u32[]{:S(2)}) async-start(bf16[16,8,640]{2,1,0:T(8,128)(2,1)} %broadcast_in_dim.49), calls=%async_computation.8 | async-start | bytes 327680 | tf_op jit(solution)/shard_map/all_to_all | solution.py:125
  9.7 0.1 pad_add_fusion
  9.8 12.4 %all-to-all-done.8 = bf16[16,8,640]{2,1,0:T(8,128)(2,1)S(1)} async-done(((bf16[16,8,640]{2,1,0:T(8,128)(2,1)}), bf16[16,8,640]{2,1,0:T(8,128)(2,1)S(1)}, u32[]{:S(2)}, u32[]{:S(2)}) %all-to-all-start.8) | async-done | bytes 163872 | tf_op jit(solution)/shard_map/all_to_all | solution.py:125
  22.1 58.1 %conditional.1 = (bf16[2,512,128]{2,1,0:T(8,128)(2,1)S(1)}) conditional(s32[]{:T(128)} %clamp.3, (bf16[16,8,640]{2,1,0:T(8,128)(2,1)S(1)}, s32[2]{0:T(128)S(1)}, s32[64,6]{0,1:T(8,128)}, s32[64,4]{0,1:T(4,128)}, bf16[2,512,576]{1,2,0:T(8,128)(2,1)}, /*index=5*/bf16[2,512,128]{2,1,0:T(8,128)(2,1)}, s32[]{:T(128)}, ...), branch_computations={%region_0.1_spmd, %region_1.2_spmd, %region_2.3_spmd, %region_3.4_... | conditional | flops 2621440 | bytes 39763192 | solution.py:135
  22.1 0.1 broadcast_in_dim.46
  22.2 11.6 %all_to_all.43 = bf16[4,4,32,640]{3,2,1,0:T(8,128)(2,1)S(1)} all-to-all(bf16[4,4,32,640]{3,2,1,0:T(8,128)(2,1)S(1)} %broadcast_in_dim.46), channel_id=1, replica_groups={{0,4,8,12},{1,5,9,13},{2,6,10,14},{3,7,11,15},{16,20,24,28},{17,21,25,2..., dimensions={0} | all-to-all | bytes 1310720 | tf_op jit(solution)/shard_map/cond/branch_3_fun/all_to_all | solution.py:113
  33.8 0.3 broadcast_in_dim.47
  34.1 0.0 copy-start.12
  34.1 0.0 copy-start.16
  34.2 0.0 copy-start.3
  34.2 22.5 %all_to_all.44 = bf16[4,4,4,32,640]{4,3,2,1,0:T(8,128)(2,1)} all-to-all(bf16[4,4,4,32,640]{4,3,2,1,0:T(8,128)(2,1)S(1)} %broadcast_in_dim.47), channel_id=1, replica_groups={{0,16,32,48},{1,17,33,49},{2,18,34,50},{3,19,35,51},{4,20,36,52},{5,21,..., dimensions={0} | all-to-all | bytes 5242880 | tf_op jit(solution)/shard_map/cond/branch_3_fun/all_to_all | solution.py:113
  56.6 8.6 %collective-permute-start.3 = (bf16[4,4,4,32,640]{4,3,2,1,0:T(8,128)(2,1)}, bf16[4,4,4,32,640]{4,3,2,1,0:T(8,128)(2,1)}, u32[]{:S(2)}, u32[]{:S(2)}) collective-permute-start(bf16[4,4,4,32,640]{4,3,2,1,0:T(8,128)(2,1)} %all_to_all.44), channel_id=1, source_target_pairs={{0,64},{1,65},{2,66},{3,67},{4,68},{5,69},{6,70},{7,71},{8,72},{9,... | collective-permute-start | bytes 7864328 | tf_op jit(solution)/shard_map/cond/branch_3_fun/ppermute | solution.py:131
  65.2 0.0 copy-done.12
  65.3 0.1 copy.47
  65.4 0.0 copy-done.16
  65.4 0.1 copy.48
  65.5 0.0 copy-done.3
  65.5 0.7 copy.49.q_ref
  66.2 3.9 %collective-permute-done.3 = bf16[4,4,4,32,640]{4,3,2,1,0:T(8,128)(2,1)} collective-permute-done((bf16[4,4,4,32,640]{4,3,2,1,0:T(8,128)(2,1)}, bf16[4,4,4,32,640]{4,3,2,1,0:T(8,128)(2,1)}, u32[]{:S(2)}, u32[]{:S(2)}) %collective-permute-start.3) | collective-permute-done | bytes 2621472 | tf_op jit(solution)/shard_map/cond/branch_3_fun/ppermute | solution.py:131
  70.1 0.0 copy-start.7
  70.1 3.1 %pad_maximum_fusion.3.kv_ref = bf16[2,16,4,32,640]{4,3,2,1,0:T(8,128)(2,1)S(1)} fusion(bf16[1,16,4,32,640]{4,3,2,1,0:T(8,128)(2,1)} %bitcast.20, bf16[1,16,4,32,640]{4,3,2,1,0:T(8,128)(2,1)} %bitcast.19), kind=kLoop, calls=%fused_computation.16 | loop fusion | flops 2621440 | bytes 10485760 | tf_op jit(solution)/shard_map/cond/branch_3_fun/stack | solution.py:132
  73.2 0.0 copy-done.7
  73.2 6.8 %attention.7 = bf16[2,512,128]{2,1,0:T(8,128)(2,1)S(1)} custom-call(s32[2]{0:T(128)S(1)} %get-tuple-element.76.place, s32[6]{0:T(128)S(1)} %fusion.6.vert, s32[4]{0:T(128)S(1)} %fusion.7.slash, bf16[2,512,576]{2,1,0:T(8,128)(2,1)S(1)} %copy.49.q_ref, bf16[2,16,4,32,640]{4,3,2,1,0:T(8,128)(2,1)S(1)} %pad_maximum_fusion.3.kv_ref, ...), custom_call_target="tpu_custom_call" | custom-call | tf_op jit(solution)/shard_map/cond/branch_3_fun/attention/pallas_call | solution.py:83
  80.3 0.0 copy-start.8
  80.3 0.7 copy-done.8
  (2 shorter events, 0.0 us)
Async XLA Ops:
  1.4 20.7 %all-to-all-start.8 = ((bf16[16,8,640]{2,1,0:T(8,128)(2,1)}), bf16[16,8,640]{2,1,0:T(8,128)(2,1)S(1)}, u32[]{:S(2)}, u32[]{:S(2)}) async-start(bf16[16,8,640]{2,1,0:T(8,128)(2,1)} %broadcast_in_dim.49), calls=%async_computation.8 | async-start | bytes 327680 | tf_op jit(solution)/shard_map/all_to_all | solution.py:125
  34.1 31.1 %copy-start.12 = (s32[64,6]{0,1:T(8,128)S(1)}, s32[64,6]{0,1:T(8,128)}, u32[]{:S(2)}) copy-start(s32[64,6]{0,1:T(8,128)} %get-tuple-element.219) | copy-start | bytes 4612 | tf_op jit(solution)/shard_map/cond
  34.1 31.2 %copy-start.16 = (s32[64,4]{0,1:T(4,128)S(1)}, s32[64,4]{0,1:T(4,128)}, u32[]{:S(2)}) copy-start(s32[64,4]{0,1:T(4,128)} %get-tuple-element.220) | copy-start | bytes 3076 | tf_op jit(solution)/shard_map/cond
  34.2 31.3 %copy-start.3 = (bf16[2,512,576]{1,2,0:T(8,128)(2,1)S(1)}, bf16[2,512,576]{1,2,0:T(8,128)(2,1)}, u32[]{:S(2)}) copy-start(bf16[2,512,576]{1,2,0:T(8,128)(2,1)} %get-tuple-element.221) | copy-start | bytes 3538948 | tf_op jit(solution)/shard_map/cond
  56.6 13.5 %collective-permute-start.3 = (bf16[4,4,4,32,640]{4,3,2,1,0:T(8,128)(2,1)}, bf16[4,4,4,32,640]{4,3,2,1,0:T(8,128)(2,1)}, u32[]{:S(2)}, u32[]{:S(2)}) collective-permute-start(bf16[4,4,4,32,640]{4,3,2,1,0:T(8,128)(2,1)} %all_to_all.44), channel_id=1, source_target_pairs={{0,64},{1,65},{2,66},{3,67},{4,68},{5,69},{6,70},{7,71},{8,72},{9,... | collective-permute-start | bytes 7864328 | tf_op jit(solution)/shard_map/cond/branch_3_fun/ppermute | solution.py:131
  70.1 3.1 %copy-start.7 = (bf16[2,512,128]{2,1,0:T(8,128)(2,1)S(1)}, bf16[2,512,128]{2,1,0:T(8,128)(2,1)}, u32[]{:S(2)}) copy-start(bf16[2,512,128]{2,1,0:T(8,128)(2,1)} %get-tuple-element.130.w_ref) | copy-start | bytes 786436 | tf_op jit(solution)/shard_map/cond
  80.3 0.7 copy-start.8

commit v3 on v2

v3 whole, which is shorter than its diff:
```python
import functools

import jax
import jax.numpy as jnp
from jax import lax
from jax.experimental import pallas as pl
from jax.experimental.pallas import tpu as pltpu
from jax.sharding import Mesh, PartitionSpec as P

TILE = 128
HEADS = 2
LAT = 512
KV = 576
WIDE = 640
ROWS = 512
BLOCKS = 4
ROW_SCALE = 192.0 ** -0.5 * 1.4426950408889634
DEAD = -1e30
STEPS = (2, 3, 4)
ALL = ("zh", "core", "y", "x", "zl")


def choose(place, vert, slash, plan_ref):
    half = place[1]
    for b in range(BLOCKS):
        i = place[0] * BLOCKS + b
        live = jnp.int32(0)
        for n in range(6):
            v = vert[n]
            live = live | jnp.where(v < i, jnp.int32(1) << v, 0)
        for n in range(4):
            v = i - slash[n]
            live = live | jnp.where(v >= 0, jnp.int32(1) << jnp.maximum(v, 0), 0)
        for n in range(12):
            plan_ref[b, n] = i
            plan_ref[BLOCKS + b, n] = i
        mine, others = jnp.int32(1), jnp.int32(0)
        for j in range(31):
            bit = (live >> j) & 1
            same = jnp.where((j >> 2) & 1 == half, bit, 0)
            plan_ref[b, mine] = jnp.where(same == 1, j, i)
            mine = mine + same
            plan_ref[BLOCKS + b, others] = jnp.where(bit - same == 1, j, i)
            others = others + bit - same
        plan_ref[b, 31] = mine
        plan_ref[BLOCKS + b, 31] = others


def choice(place, vert, slash):
    smem = pl.BlockSpec(memory_space=pltpu.SMEM)
    return pl.pallas_call(
        choose,
        out_shape=jax.ShapeDtypeStruct((2 * BLOCKS, 32), jnp.int32),
        in_specs=[smem, smem, smem],
        out_specs=smem,
        name="choice",
    )(place, vert, slash)


def steps(most):
    ends = [n for n in STEPS if n < most] + [most]
    return list(zip([0] + ends, ends))


def scored(b, under, pairs, first, plan, row, half, q_ref, kv_ref, s_ref):
    q = jnp.concatenate([q_ref[h, :, pl.ds(pl.multiple_of(b * TILE, TILE), TILE)].T for h in range(HEADS)], axis=0)

    def pair(p, width):
        pieces = []
        for n in range(2):
            tile = plan[row, 2 * p + n]
            zh, y = tile >> 3, tile & 3
            start, step = jnp.where(half == 0, 4 * y, y), jnp.where(half == 0, 1, 4)
            pieces += [kv_ref[start + step * m, zh, :, :width] for m in range(4)]
        return jnp.concatenate(pieces, axis=0)

    top = None
    for p in range(pairs):
        s = lax.dot_general(q, pair(p, KV), (((1,), (1,)), ((), ())), preferred_element_type=jnp.float32)
        s = s * ROW_SCALE
        left, right = s[:, :TILE], s[:, TILE:]
        if first and p == 0:
            at = lax.broadcasted_iota(jnp.int32, (HEADS * TILE, TILE), 0) & (TILE - 1)
            left = jnp.where(lax.broadcasted_iota(jnp.int32, (HEADS * TILE, TILE), 1) <= at, left, DEAD)
        if p >= under:
            left = left + jnp.where(2 * p < plan[row, 31], 0.0, DEAD) if p > under else left
            right = right + jnp.where(2 * p + 1 < plan[row, 31], 0.0, DEAD)
        s_ref[:, 2 * p * TILE : (2 * p + 1) * TILE] = left
        s_ref[:, (2 * p + 1) * TILE : (2 * p + 2) * TILE] = right
        t = jnp.maximum(jnp.max(left, axis=1, keepdims=True), jnp.max(right, axis=1, keepdims=True))
        top = t if top is None else jnp.maximum(top, t)
    return top, pair


def summed(pairs, pair, top, total, acc, s_ref):
    for p in range(pairs):
        w = jnp.exp2(s_ref[:, p * 2 * TILE : (p + 1) * 2 * TILE] - top)
        total = total + jnp.sum(w, axis=1, keepdims=True)
        acc = acc + jnp.dot(w.astype(jnp.bfloat16), pair(p, LAT), preferred_element_type=jnp.float32)
    return total, acc


def attend_own(most, place, plan, q_ref, kv_ref, acc_ref, top_ref, total_ref, s_ref):
    def tile(b, _):
        held = plan[b, 31]
        for under, pairs in steps(most):
            @pl.when((held > 2 * under) & (held <= 2 * pairs))
            def _(under=under, pairs=pairs):
                top, pair = scored(b, under, pairs, True, plan, b, place[1], q_ref, kv_ref, s_ref)
                total = jnp.zeros((HEADS * TILE, 1), jnp.float32)
                acc = jnp.zeros((HEADS * TILE, LAT), jnp.float32)
                total, acc = summed(pairs, pair, top, total, acc, s_ref)
                acc_ref[b] = acc
                top_ref[b] = jnp.broadcast_to(top, (HEADS * TILE, TILE))
                total_ref[b] = jnp.broadcast_to(total, (HEADS * TILE, TILE))
        return 0

    lax.fori_loop(0, BLOCKS, tile, 0)


def attend_other(most, place, plan, q_ref, kv_ref, acc_ref, top_ref, total_ref, w_ref, out_ref, s_ref):
    def tile(b, _):
        held = plan[BLOCKS + b, 31]
        for under, pairs in [(-1, 0)] + steps(most):
            @pl.when((held > 2 * under) & (held <= 2 * pairs))
            def _(under=under, pairs=pairs):
                total, acc = total_ref[b, :, :1], acc_ref[b]
                if pairs:
                    top, pair = scored(b, under, pairs, False, plan, BLOCKS + b, 1 - place[1], q_ref, kv_ref, s_ref)
                    top = jnp.maximum(top, top_ref[b, :, :1])
                    fall = jnp.exp2(top_ref[b, :, :1] - top)
                    total, acc = summed(pairs, pair, top, fall * total, fall * acc, s_ref)
                latent = (acc / total).astype(jnp.bfloat16)
                for h in range(HEADS):
                    up = jnp.dot(latent[h * TILE : (h + 1) * TILE], w_ref[h], preferred_element_type=jnp.float32)
                    out_ref[h, pl.ds(pl.multiple_of(b * TILE, TILE), TILE), :] = up.astype(jnp.bfloat16)
        return 0

    lax.fori_loop(0, BLOCKS, tile, 0)


smem = pl.BlockSpec(memory_space=pltpu.SMEM)
vmem = pl.BlockSpec(memory_space=pltpu.VMEM)


def own_half(place, plan, q, kv):
    most = min(6, 2 * kv.shape[1])
    part = jax.ShapeDtypeStruct((BLOCKS, HEADS * TILE, TILE), jnp.float32)
    return pl.pallas_call(
        functools.partial(attend_own, most),
        out_shape=(jax.ShapeDtypeStruct((BLOCKS, HEADS * TILE, LAT), jnp.float32), part, part),
        in_specs=[smem, smem, vmem, vmem],
        out_specs=(vmem, vmem, vmem),
        scratch_shapes=[pltpu.VMEM((HEADS * TILE, 2 * most * TILE), jnp.float32)],
        compiler_params=pltpu.CompilerParams(vmem_limit_bytes=16 * 1024 * 1024),
        cost_estimate=pl.CostEstimate(flops=1 << 31, bytes_accessed=1 << 22, transcendentals=1 << 20),
        name="own_half",
    )(place, plan, q, kv)


def other_half(place, plan, q, kv, parts, w):
    most = min(6, 2 * kv.shape[1])
    return pl.pallas_call(
        functools.partial(attend_other, most),
        out_shape=jax.ShapeDtypeStruct((HEADS, ROWS, 128), jnp.bfloat16),
        in_specs=[smem, smem, vmem, vmem, vmem, vmem, vmem, vmem],
        out_specs=vmem,
        scratch_shapes=[pltpu.VMEM((HEADS * TILE, 2 * most * TILE), jnp.float32)],
        compiler_params=pltpu.CompilerParams(vmem_limit_bytes=16 * 1024 * 1024),
        cost_estimate=pl.CostEstimate(flops=1 << 31, bytes_accessed=1 << 22, transcendentals=1 << 20),
        name="other_half",
    )(place, plan, q, kv, *parts, w)


def device_at(zh, core, y, x, zl):
    return (((zh * 2 + core) * 4 + y) * 4 + x) * 4 + zl


def lines(swapped):
    out = []
    for zh in range(4):
        for core in range(2):
            for at in range(4):
                for zl in range(4):
                    along_x = (core == 0) != swapped
                    out.append([device_at(zh, core, *((at, n) if along_x else (n, at)), zl) for n in range(4)])
    return out


def to_all(block, groups):
    return lax.all_to_all(jnp.broadcast_to(block[None], (4, *block.shape)), ALL, 0, 0, axis_index_groups=groups)


other_core = [(device_at(a, c, 0, 0, 0) + n, device_at(a, 1 - c, 0, 0, 0) + n) for a in range(4) for c in range(2) for n in range(64)]


def on_device(queries, kv_latent, vert_tiles, slash_offsets, w_uv):
    zh, core = lax.axis_index("zh"), lax.axis_index("core")
    grp_at = (lax.axis_index("y") * 4 + lax.axis_index("x")) * 4 + lax.axis_index("zl")
    place = jnp.stack([zh * 2 + core, core]).astype(jnp.int32)
    rows = jnp.pad(kv_latent, ((0, 0), (0, WIDE - KV)))
    column = lax.all_to_all(jnp.broadcast_to(rows[None], (16, 8, WIDE)), ("zh", "zl"), 0, 0)

    plan = choice(place, vert_tiles[grp_at], slash_offsets[grp_at])
    turned = queries.transpose(0, 2, 1)

    def plane(depth, column):
        block = column[: 4 * depth].reshape(depth, 32, WIDE)
        block = to_all(block, lines(False))
        own = to_all(block, lines(True)).reshape(16, depth, 32, WIDE)
        other = lax.ppermute(own, ALL, other_core)
        parts = own_half(place, plan, turned, own)
        return other_half(place, plan, turned, other, parts, w_uv)

    return lax.switch(zh, [functools.partial(plane, depth) for depth in range(1, 5)], column)


def solution(mesh):
    fine = Mesh(mesh.devices.reshape(4, 2, 4, 4, 4), ALL)
    ctx, grp = ("zh", "core"), ("y", "x", "zl")
    placed = (P(grp, ctx, None), P(ctx + grp, None), P(), P(), P(grp, None, None))
    return jax.shard_map(
        on_device, mesh=fine, in_specs=placed, out_specs=P(grp, ctx, None), check_vma=False
    )
```

time: 81.3 us -> 77.5 us (0.953)
  waiting for transfers between devices: 16.3 us -> 8.55 us
  Pallas kernels: 6.76 us -> 12.6 us
  other arithmetic: 3.19 us -> 0.07 us
  local copies, waits for them, and re-layouts: 3.41 us -> 4.61 us
    pallas_call x1 -> x3, Pallas kernels: 6.76 us -> 12.6 us  [the longest x1 6.46 us: other_half(): pl.pallas_call(functools.partial(attend_other, most), out_shape=jax.Shape...]
    all_to_all x1, waiting for transfers between devices: 12.4 us -> 7.94 us  [on_device(): lax.all_to_all(jnp.broadcast_to(rows[None], (16, 8, WIDE)), ('zh', 'zl'),...]
    ppermute x1, waiting for transfers between devices: 3.89 us -> 0.61 us  [plane(): other = lax.ppermute(own, ALL, other_core)]
    another operation x1 -> x0, other arithmetic: 3.11 us -> none  [plane(): kv = jnp.stack([own, other]).reshape(2, 16, depth, 32, WIDE)]
    dynamic_slice x0 -> x2, local copies, waits for them, and re-layouts: none -> 2.12 us  [on_device(): plan = choice(place, vert_tiles[grp_at], slash_offsets[grp_at])]
    another operation x3 -> x0, local copies, waits for them, and re-layouts: 0.91 us -> none
  transfers between devices with their start and end apart: 2 -> 2, of which waited for: 2 -> 2; matrix products, arithmetic and copies ran while one was open for 1% -> 3% of each run, Pallas kernels for 0% -> 8%
where the time goes in v3:
time: 77.5 us; the launch traced here: 77.1 us
  blocking collectives  34 us (44%)
  starting transfers between devices  16.9 us (22%)
  Pallas kernels  12.6 us (16%)
  waiting for transfers between devices  8.55 us (11%)
  local copies, waits for them, and re-layouts  4.61 us (6%)
    all_to_all x2, blocking collectives, to_all(): lax.all_to_all(jnp.broadcast_to(block[None], (4, *block.shape)), ALL, 0,...  34 us
    ppermute x1, starting transfers between devices, plane(): other = lax.ppermute(own, ALL, other_core)  8.61 us
    all_to_all x1, starting transfers between devices, on_device(): lax.all_to_all(jnp.broadcast_to(rows[None], (16, 8, WIDE)), ('zh', 'zl'),...  8.29 us
    all_to_all x1, waiting for transfers between devices, on_device(): lax.all_to_all(jnp.broadcast_to(rows[None], (16, 8, WIDE)), ('zh', 'zl'),...  7.94 us
    pallas_call x1, Pallas kernels, other_half(): pl.pallas_call(functools.partial(attend_other, most), out_shape=jax.Shape...  6.46 us
    pallas_call x1, Pallas kernels, own_half(): pl.pallas_call(functools.partial(attend_own, most), out_shape=(jax.ShapeD...  3.87 us
    pallas_call x1, Pallas kernels, choice(): pl.pallas_call(choose, out_shape=jax.ShapeDtypeStruct((2 * BLOCKS, 32), j...  2.3 us
    dynamic_slice x2, local copies, waits for them, and re-layouts, on_device(): plan = choice(place, vert_tiles[grp_at], slash_offsets[grp_at])  2.12 us
  transfers between devices with their start and end apart: 2, of which 2 were waited for; matrix products, arithmetic and copies ran while one was open for 3% of the time, Pallas kernels for 8%

profile of v3, /device:TPU:481, one launch (start us, length us, event | category | flops | bytes accessed | tf_op | source)
XLA Modules:
  0.0 77.1 jit_solution(9923700224877575658)
XLA Ops:
  0.0 0.0 copy-start
  0.0 0.7 pad.4
  0.7 0.7 broadcast_in_dim.49
  1.4 8.3 %all-to-all-start.8 = ((bf16[16,8,640]{2,1,0:T(8,128)(2,1)}), bf16[16,8,640]{2,1,0:T(8,128)(2,1)S(1)}, u32[]{:S(2)}, u32[]{:S(2)}) async-start(bf16[16,8,640]{2,1,0:T(8,128)(2,1)} %broadcast_in_dim.49), calls=%async_computation.8 | async-start | bytes 327680 | tf_op jit(solution)/shard_map/all_to_all | solution.py:202
  9.7 0.0 copy-done
  9.7 0.7 dynamic-slice_reduce_fusion.vert
  10.4 1.4 %dynamic-slice_reduce_fusion.1.slash = s32[4]{0:T(128)} fusion(s32[64,4]{0,1:T(4,128)} %param.12, s32[]{:T(128)S(6)} %select_n.4), kind=kLoop, calls=%fused_computation.2 | loop fusion | bytes 36 | tf_op jit(solution)/shard_map/dynamic_slice | solution.py:204
  11.8 0.1 pad_add_fusion.place
  11.9 2.3 %choice.1 = s32[8,32]{1,0:T(8,128)S(1)} custom-call(s32[2]{0:T(128)S(1)} %pad_add_fusion.place, s32[6]{0:T(128)} %dynamic-slice_reduce_fusion.vert, s32[4]{0:T(128)} %dynamic-slice_reduce_fusion.1.slash), custom_call_target="tpu_custom_call" | custom-call | tf_op jit(solution)/shard_map/choice/pallas_call | solution.py:51
  14.2 7.9 %all-to-all-done.8 = bf16[16,8,640]{2,1,0:T(8,128)(2,1)S(1)} async-done(((bf16[16,8,640]{2,1,0:T(8,128)(2,1)}), bf16[16,8,640]{2,1,0:T(8,128)(2,1)S(1)}, u32[]{:S(2)}, u32[]{:S(2)}) %all-to-all-start.8) | async-done | bytes 163872 | tf_op jit(solution)/shard_map/all_to_all | solution.py:202
  22.1 54.2 %conditional.1 = (bf16[2,512,128]{2,1,0:T(8,128)(2,1)S(1)}) conditional(s32[]{:T(128)} %clamp.3, (bf16[16,8,640]{2,1,0:T(8,128)(2,1)S(1)}, s32[2]{0:T(128)S(1)}, s32[8,32]{1,0:T(8,128)S(1)}, bf16[2,576,512]{2,1,0:T(8,128)(2,1)}, bf16[2,512,128]{2,1,0:T(8,128)(2,1)}) %tuple.26, (bf16[16,8,640]{2,1,0:T(8,128)(2,1)S(1)}, ...), branch_computations={%region_0.1_spmd, %region_1.2_spmd, %region_2.3_spmd, %region_3.4_... | conditional | flops 4294967296 | bytes 35291240 | solution.py:215
  22.1 0.1 broadcast_in_dim.46
  22.2 11.6 %all_to_all.43 = bf16[4,4,32,640]{3,2,1,0:T(8,128)(2,1)S(1)} all-to-all(bf16[4,4,32,640]{3,2,1,0:T(8,128)(2,1)S(1)} %broadcast_in_dim.46), channel_id=1, replica_groups={{0,4,8,12},{1,5,9,13},{2,6,10,14},{3,7,11,15},{16,20,24,28},{17,21,25,2..., dimensions={0} | all-to-all | bytes 1310720 | tf_op jit(solution)/shard_map/cond/branch_3_fun/all_to_all | solution.py:191
  33.8 0.3 broadcast_in_dim.47
  34.2 0.0 copy-start.4
  34.2 22.3 %all_to_all.44 = bf16[4,4,4,32,640]{4,3,2,1,0:T(8,128)(2,1)S(1)} all-to-all(bf16[4,4,4,32,640]{4,3,2,1,0:T(8,128)(2,1)S(1)} %broadcast_in_dim.47), channel_id=1, replica_groups={{0,16,32,48},{1,17,33,49},{2,18,34,50},{3,19,35,51},{4,20,36,52},{5,21,..., dimensions={0} | all-to-all | bytes 5242880 | tf_op jit(solution)/shard_map/cond/branch_3_fun/all_to_all | solution.py:191
  56.5 8.6 %collective-permute-start.2 = (bf16[16,4,32,640]{3,2,1,0:T(8,128)(2,1)S(1)}, bf16[16,4,32,640]{3,2,1,0:T(8,128)(2,1)S(1)}, u32[]{:S(2)}, u32[]{:S(2)}) collective-permute-start(bf16[16,4,32,640]{3,2,1,0:T(8,128)(2,1)S(1)} %bitcast.13), channel_id=1, source_target_pairs={{0,64},{1,65},{2,66},{3,67},{4,68},{5,69},{6,70},{7,71},{8,72},{9,... | collective-permute-start | bytes 7864328 | tf_op jit(solution)/shard_map/cond/branch_3_fun/ppermute | solution.py:211
  65.1 0.0 copy-done.4
  65.1 0.0 copy-start.8
  65.2 3.9 %own_half.7 = (f32[4,256,512]{2,1,0:T(8,128)S(1)}, f32[4,256,128]{2,1,0:T(8,128)S(1)}, f32[4,256,128]{2,1,0:T(8,128)S(1)}) custom-call(s32[2]{0:T(128)S(1)} %get-tuple-element.74.place, s32[8,32]{1,0:T(8,128)S(1)} %get-tuple-element.75.plan, bf16[2,576,512]{2,1,0:T(8,128)(2,1)S(1)} %copy-done.4, bf16[16,4,32,640]{3,2,1,0:T(8,128)(2,1)S(1)} %bitcast.14), custom_call_target="tpu_custom_call" | custom-call | flops 2147483648 | bytes 4194304 | tf_op jit(solution)/shard_map/cond/branch_3_fun/own_half/pallas_call | solution.py:149
  69.0 0.6 collective-permute-done.2.kv_ref
  69.7 0.0 copy-done.8
  69.7 6.5 %other_half.7 = bf16[2,512,128]{2,1,0:T(8,128)(2,1)S(1)} custom-call(s32[2]{0:T(128)S(1)} %get-tuple-element.74.place, s32[8,32]{1,0:T(8,128)S(1)} %get-tuple-element.75.plan, bf16[2,576,512]{2,1,0:T(8,128)(2,1)S(1)} %copy-done.4, bf16[16,4,32,640]{3,2,1,0:T(8,128)(2,1)S(1)} %collective-permute-done.2.kv_ref, f32[4,256,512]{2,1,0:T(8,128)S(1)} %get-tuple-element.78.acc_ref, ...), custom_call_target="tpu_custom_call" | custom-call | flops 2147483648 | bytes 4194304 | tf_op jit(solution)/shard_map/cond/branch_3_fun/other_half/pallas_call | solution.py:163
  76.4 0.0 copy-start.9
  76.4 0.7 copy-done.9
Async XLA Ops:
  0.0 9.7 %copy-start = (s32[64,6]{0,1:T(8,128)S(1)}, s32[64,6]{0,1:T(8,128)}, u32[]{:S(2)}) copy-start(s32[64,6]{0,1:T(8,128)} %param.11) | copy-start | bytes 4612
  1.4 20.7 %all-to-all-start.8 = ((bf16[16,8,640]{2,1,0:T(8,128)(2,1)}), bf16[16,8,640]{2,1,0:T(8,128)(2,1)S(1)}, u32[]{:S(2)}, u32[]{:S(2)}) async-start(bf16[16,8,640]{2,1,0:T(8,128)(2,1)} %broadcast_in_dim.49), calls=%async_computation.8 | async-start | bytes 327680 | tf_op jit(solution)/shard_map/all_to_all | solution.py:202
  34.2 31.0 %copy-start.4 = (bf16[2,576,512]{2,1,0:T(8,128)(2,1)S(1)}, bf16[2,576,512]{2,1,0:T(8,128)(2,1)}, u32[]{:S(2)}) copy-start(bf16[2,576,512]{2,1,0:T(8,128)(2,1)} %get-tuple-element.76.q_ref) | copy-start | bytes 3538948 | tf_op jit(solution)/shard_map/cond
  56.5 13.1 %collective-permute-start.2 = (bf16[16,4,32,640]{3,2,1,0:T(8,128)(2,1)S(1)}, bf16[16,4,32,640]{3,2,1,0:T(8,128)(2,1)S(1)}, u32[]{:S(2)}, u32[]{:S(2)}) collective-permute-start(bf16[16,4,32,640]{3,2,1,0:T(8,128)(2,1)S(1)} %bitcast.13), channel_id=1, source_target_pairs={{0,64},{1,65},{2,66},{3,67},{4,68},{5,69},{6,70},{7,71},{8,72},{9,... | collective-permute-start | bytes 7864328 | tf_op jit(solution)/shard_map/cond/branch_3_fun/ppermute | solution.py:211
  65.1 4.5 %copy-start.8 = (bf16[2,512,128]{2,1,0:T(8,128)(2,1)S(1)}, bf16[2,512,128]{2,1,0:T(8,128)(2,1)}, u32[]{:S(2)}) copy-start(bf16[2,512,128]{2,1,0:T(8,128)(2,1)} %get-tuple-element.90.w_ref) | copy-start | bytes 786436 | tf_op jit(solution)/shard_map/cond
  76.4 0.7 copy-start.9

commit v4 on v3

v4 whole, which is shorter than its diff:
```python
import functools

import jax
import jax.numpy as jnp
from jax import lax
from jax.experimental import pallas as pl
from jax.experimental.pallas import tpu as pltpu
from jax.sharding import Mesh, PartitionSpec as P

TILE = 128
HEADS = 2
LAT = 512
KV = 576
ROWS = 512
BLOCKS = 4
ROW_SCALE = 192.0 ** -0.5 * 1.4426950408889634
DEAD = -1e30
OWN_PAIRS = 4
OTHER_PAIRS = 4
ALL = ("zh", "core", "y", "x", "zl")


def choose(place, vert, slash, plan_ref):
    half = place[1]
    for b in range(BLOCKS):
        i = place[0] * BLOCKS + b
        live = jnp.int32(0)
        for n in range(6):
            v = vert[n]
            live = live | jnp.where(v < i, jnp.int32(1) << v, 0)
        for n in range(4):
            v = i - slash[n]
            live = live | jnp.where(v >= 0, jnp.int32(1) << jnp.maximum(v, 0), 0)
        for n in range(12):
            plan_ref[b, n] = i
            plan_ref[BLOCKS + b, n] = i
        mine, others = jnp.int32(1), jnp.int32(0)
        for j in range(31):
            bit = (live >> j) & 1
            same = jnp.where((j >> 2) & 1 == half, bit, 0)
            plan_ref[b, mine] = jnp.where(same == 1, j, i)
            mine = mine + same
            plan_ref[BLOCKS + b, others] = jnp.where(bit - same == 1, j, i)
            others = others + bit - same
        plan_ref[b, 31] = mine
        plan_ref[BLOCKS + b, 31] = others


def choice(place, vert, slash):
    smem = pl.BlockSpec(memory_space=pltpu.SMEM)
    return pl.pallas_call(
        choose,
        out_shape=jax.ShapeDtypeStruct((2 * BLOCKS, 32), jnp.int32),
        in_specs=[smem, smem, smem],
        out_specs=smem,
        name="choice",
    )(place, vert, slash)


def pair_of(p, plan, row, half, kv_ref, rotary):
    lane = lax.broadcasted_iota(jnp.int32, (16, TILE), 1)
    sides = [(lane < 64).astype(jnp.bfloat16), (lane >= 64).astype(jnp.bfloat16)]
    pieces = []
    for n in range(2):
        tile = plan[row, 2 * p + n]
        zh, y = tile >> 3, tile & 3
        start, step = jnp.where(half == 0, 4 * y, y), jnp.where(half == 0, 1, 4)
        for m in range(4):
            at = start + step * m
            parts = [kv_ref[at, zh, 32 * t : 32 * t + 32, :] for t in range(4)]
            if rotary:
                both = kv_ref[at, zh, 128:, :]
                parts.append(jnp.concatenate([both * side for side in sides], axis=0))
            pieces.append(jnp.concatenate(parts, axis=1))
    return jnp.concatenate(pieces, axis=0)


def scores(q, p, own_tile, plan, row, half, kv_ref):
    s = lax.dot_general(
        q, pair_of(p, plan, row, half, kv_ref, True), (((1,), (1,)), ((), ())), preferred_element_type=jnp.float32
    )
    s = s * ROW_SCALE
    left, right = s[:, :TILE], s[:, TILE:]
    if own_tile:
        at = lax.broadcasted_iota(jnp.int32, (HEADS * TILE, TILE), 0) & (TILE - 1)
        left = jnp.where(lax.broadcasted_iota(jnp.int32, (HEADS * TILE, TILE), 1) <= at, left, DEAD)
    else:
        left = left + jnp.where(2 * p < plan[row, 31], 0.0, DEAD)
    right = right + jnp.where(2 * p + 1 < plan[row, 31], 0.0, DEAD)
    return jnp.concatenate([left, right], axis=1)


def wide(column, times):
    return jnp.concatenate([column] * times, axis=1)


def every_lane(column):
    return jnp.broadcast_to(column, (HEADS * TILE, TILE))


def weighted(s, top, p, plan, row, half, kv_ref):
    w = jnp.exp2(s - wide(top, 2))
    values = pair_of(p, plan, row, half, kv_ref, False)
    return w[:, :TILE] + w[:, TILE:], jnp.dot(w.astype(jnp.bfloat16), values, preferred_element_type=jnp.float32)


def many(q, pairs, own, plan, row, half, kv_ref, s_ref, top, total, acc):
    start, largest = top, None
    for p in range(pairs):
        s = scores(q, p, own and p == 0, plan, row, half, kv_ref)
        s_ref[:, p * 2 * TILE : (p + 1) * 2 * TILE] = s
        t = jnp.max(s, axis=1, keepdims=True)
        largest = t if largest is None else jnp.maximum(largest, t)
    top = every_lane(largest)
    if start is not None:
        top = jnp.maximum(start, top)
        fall = jnp.exp2(start - top)
        total, acc = fall * total, wide(fall, LAT // TILE) * acc
    add = None
    for p in range(pairs):
        t, a = weighted(s_ref[:, p * 2 * TILE : (p + 1) * 2 * TILE], top, p, plan, row, half, kv_ref)
        add, acc = (t if add is None else add + t), (a if acc is None else acc + a)
    add = every_lane(jnp.sum(add, axis=1, keepdims=True))
    return top, add if total is None else total + add, acc


def rest(pairs, plan, first_row, half, kv_ref, q_ref, acc_ref, top_ref, total_ref):
    def tile(b, _):
        row = first_row + b

        def one(p, _):
            s = scores(q_ref[b], p, False, plan, row, half, kv_ref)
            top = jnp.maximum(every_lane(jnp.max(s, axis=1, keepdims=True)), top_ref[b])
            fall = jnp.exp2(top_ref[b] - top)
            t, a = weighted(s, top, p, plan, row, half, kv_ref)
            acc_ref[b] = wide(fall, LAT // TILE) * acc_ref[b] + a
            total_ref[b] = fall * total_ref[b] + every_lane(jnp.sum(t, axis=1, keepdims=True))
            top_ref[b] = top
            return 0

        return lax.fori_loop(pairs, (plan[row, 31] + 1) >> 1, one, 0)

    lax.fori_loop(0, BLOCKS, tile, 0)


def attend_own(pairs, more, place, plan, turned_ref, kv_ref, q_ref, acc_ref, top_ref, total_ref, s_ref):
    for b in range(BLOCKS):
        turned = [turned_ref[h, :, b * TILE : (b + 1) * TILE] for h in range(HEADS)]
        q = jnp.concatenate([jnp.concatenate([t, t[LAT:]], axis=0).T for t in turned], axis=0)
        q_ref[b] = q
        top, total, acc = many(q, pairs, True, plan, b, place[1], kv_ref, s_ref.at[b % 2], None, None, None)
        acc_ref[b] = acc
        top_ref[b] = top
        total_ref[b] = total
    if more:
        rest(pairs, plan, 0, place[1], kv_ref, q_ref, acc_ref, top_ref, total_ref)


def attend_other(pairs, more, place, plan, kv_ref, q_ref, acc_in, top_in, total_in, w_ref, out_ref, s_ref, latent_ref, *state):
    half = 1 - place[1]
    if more:
        for held, given in zip(state, (acc_in, top_in, total_in)):
            held[...] = given[...]
        rest(pairs, plan, BLOCKS, half, kv_ref, q_ref, *state)
    acc_ref, top_ref, total_ref = state or (acc_in, top_in, total_in)
    for b in range(BLOCKS):
        top, total, acc = many(
            q_ref[b], pairs, False, plan, BLOCKS + b, half, kv_ref, s_ref.at[b % 2], top_ref[b], total_ref[b], acc_ref[b]
        )
        latent_ref[b] = (acc * wide(1.0 / total, LAT // TILE)).astype(jnp.bfloat16)
    for h in range(HEADS):
        latent = jnp.concatenate([latent_ref[b, h * TILE : (h + 1) * TILE] for b in range(BLOCKS)], axis=0)
        up = jnp.dot(latent, w_ref[h], preferred_element_type=jnp.float32)
        out_ref[h] = up.astype(jnp.bfloat16)


smem = pl.BlockSpec(memory_space=pltpu.SMEM)
vmem = pl.BlockSpec(memory_space=pltpu.VMEM)


def pack(depth, column_ref, block_ref):
    for zh in range(depth):
        rows = jnp.concatenate([column_ref[4 * zh + n].astype(jnp.float32) for n in range(4)], axis=0)
        rotary = jnp.concatenate([rows[:16, LAT:], rows[16:, LAT:]], axis=1)
        block = jnp.concatenate([rows[:, n * TILE : (n + 1) * TILE] for n in range(4)] + [rotary], axis=0)
        block = block.astype(jnp.bfloat16)
        for to in range(4):
            block_ref[to, zh] = block


def packed(depth, column):
    return pl.pallas_call(
        functools.partial(pack, depth),
        out_shape=jax.ShapeDtypeStruct((4, depth, 144, TILE), jnp.bfloat16),
        in_specs=[vmem],
        out_specs=vmem,
        name="packed",
    )(column)


part = jax.ShapeDtypeStruct((BLOCKS, HEADS * TILE, TILE), jnp.float32)
accumulated = (jax.ShapeDtypeStruct((BLOCKS, HEADS * TILE, LAT), jnp.float32), part, part)


def own_half(place, plan, q, kv):
    most = min(6, 2 * kv.shape[1])
    pairs = min(OWN_PAIRS, most)
    return pl.pallas_call(
        functools.partial(attend_own, pairs, most > pairs),
        out_shape=(jax.ShapeDtypeStruct((BLOCKS, HEADS * TILE, LAT + TILE), jnp.bfloat16), *accumulated),
        in_specs=[smem, smem, vmem, vmem],
        out_specs=(vmem, vmem, vmem, vmem),
        scratch_shapes=[pltpu.VMEM((2, HEADS * TILE, 2 * pairs * TILE), jnp.float32)],
        compiler_params=pltpu.CompilerParams(vmem_limit_bytes=16 * 1024 * 1024),
        cost_estimate=pl.CostEstimate(flops=1 << 31, bytes_accessed=1 << 22, transcendentals=1 << 20),
        name="own_half",
    )(place, plan, q, kv)


def other_half(place, plan, kv, parts, w):
    most = min(6, 2 * kv.shape[1])
    pairs = min(OTHER_PAIRS, most)
    return pl.pallas_call(
        functools.partial(attend_other, pairs, most > pairs),
        out_shape=jax.ShapeDtypeStruct((HEADS, ROWS, 128), jnp.bfloat16),
        in_specs=[smem, smem, vmem, vmem, vmem, vmem, vmem, vmem],
        out_specs=vmem,
        scratch_shapes=[
            pltpu.VMEM((2, HEADS * TILE, 2 * pairs * TILE), jnp.float32),
            pltpu.VMEM((BLOCKS, HEADS * TILE, LAT), jnp.bfloat16),
            *(pltpu.VMEM(a.shape, a.dtype) for a in accumulated if most > pairs),
        ],
        compiler_params=pltpu.CompilerParams(vmem_limit_bytes=16 * 1024 * 1024),
        cost_estimate=pl.CostEstimate(flops=1 << 31, bytes_accessed=1 << 22, transcendentals=1 << 20),
        name="other_half",
    )(place, plan, kv, *parts, w)


def device_at(zh, core, y, x, zl):
    return (((zh * 2 + core) * 4 + y) * 4 + x) * 4 + zl


def lines(swapped):
    out = []
    for zh in range(4):
        for core in range(2):
            for at in range(4):
                for zl in range(4):
                    along_x = (core == 0) != swapped
                    out.append([device_at(zh, core, *((at, n) if along_x else (n, at)), zl) for n in range(4)])
    return out


def to_all(blocks, groups):
    return lax.all_to_all(blocks, ALL, 0, 0, axis_index_groups=groups)


other_core = [(device_at(a, c, 0, 0, 0) + n, device_at(a, 1 - c, 0, 0, 0) + n) for a in range(4) for c in range(2) for n in range(64)]


def on_device(queries, kv_latent, vert_tiles, slash_offsets, w_uv):
    zh, core = lax.axis_index("zh"), lax.axis_index("core")
    grp_at = (lax.axis_index("y") * 4 + lax.axis_index("x")) * 4 + lax.axis_index("zl")
    place = jnp.stack([zh * 2 + core, core]).astype(jnp.int32)
    column = lax.all_to_all(jnp.broadcast_to(kv_latent[None], (16, 8, KV)), ("zh", "zl"), 0, 0)
    plan = choice(place, vert_tiles[grp_at], slash_offsets[grp_at])
    turned = queries.transpose(0, 2, 1)

    def plane(depth, column):
        block = to_all(packed(depth, column), lines(False))
        own = to_all(jnp.broadcast_to(block[None], (4, *block.shape)), lines(True)).reshape(16, depth, 144, TILE)
        other = lax.ppermute(own, ALL, other_core)
        parts = own_half(place, plan, turned, own)
        return other_half(place, plan, other, parts, w_uv)

    return lax.switch(zh, [functools.partial(plane, depth) for depth in range(1, 5)], column)


def solution(mesh):
    fine = Mesh(mesh.devices.reshape(4, 2, 4, 4, 4), ALL)
    ctx, grp = ("zh", "core"), ("y", "x", "zl")
    placed = (P(grp, ctx, None), P(ctx + grp, None), P(), P(), P(grp, None, None))
    return jax.shard_map(
        on_device, mesh=fine, in_specs=placed, out_specs=P(grp, ctx, None), check_vma=False
    )
```

time: 77.5 us -> 75.9 us (0.979)
  blocking collectives: 34 us -> 32.4 us
    all_to_all x2, blocking collectives: 34 us -> 32.4 us  [to_all(): return lax.all_to_all(blocks, ALL, 0, 0, axis_index_groups=groups)]
    broadcast_in_dim x3 -> x2, local copies, waits for them, and re-layouts: 1.06 us -> 1.84 us  [the longest x1 1.39 us: on_device(): jnp.broadcast_to(kv_latent[None], (16, 8, KV))]
    pallas_call x2 -> x3, Pallas kernels: 10.3 us -> 10.5 us  [the longest x1 5.2 us: other_half(): pl.pallas_call(functools.partial(attend_other, pairs, most > pairs), out_...]
  transfers between devices with their start and end apart: 2 -> 2, of which waited for: 2 -> 1; matrix products, arithmetic and copies ran while one was open for 3% -> 3% of each run, Pallas kernels for 8% -> 9%
where the time goes in v4:
time: 75.9 us; the launch traced here: 75.5 us
  blocking collectives  32.4 us (43%)
  starting transfers between devices  17.2 us (23%)
  Pallas kernels  12.8 us (17%)
  waiting for transfers between devices  7.97 us (11%)
  local copies, waits for them, and re-layouts  4.64 us (6%)
    all_to_all x2, blocking collectives, to_all(): return lax.all_to_all(blocks, ALL, 0, 0, axis_index_groups=groups)  32.4 us
    ppermute x1, starting transfers between devices, plane(): other = lax.ppermute(own, ALL, other_core)  8.87 us
    all_to_all x1, starting transfers between devices, on_device(): lax.all_to_all(jnp.broadcast_to(kv_latent[None], (16, 8, KV)), ('zh', 'zl...  8.29 us
    all_to_all x1, waiting for transfers between devices, on_device(): lax.all_to_all(jnp.broadcast_to(kv_latent[None], (16, 8, KV)), ('zh', 'zl...  7.97 us
    pallas_call x1, Pallas kernels, other_half(): pl.pallas_call(functools.partial(attend_other, pairs, most > pairs), out_...  5.2 us
    pallas_call x1, Pallas kernels, own_half(): pl.pallas_call(functools.partial(attend_own, pairs, most > pairs), out_sh...  4.44 us
    pallas_call x1, Pallas kernels, choice(): pl.pallas_call(choose, out_shape=jax.ShapeDtypeStruct((2 * BLOCKS, 32), j...  2.3 us
    dynamic_slice x2, local copies, waits for them, and re-layouts, on_device(): plan = choice(place, vert_tiles[grp_at], slash_offsets[grp_at])  2.09 us
  transfers between devices with their start and end apart: 2, of which 1 were waited for; matrix products, arithmetic and copies ran while one was open for 3% of the time, Pallas kernels for 9%

profile of v4, /device:TPU:481, one launch (start us, length us, event | category | flops | bytes accessed | tf_op | source)
XLA Modules:
  0.0 75.5 jit_solution(9163434120040104615)
XLA Ops:
  0.0 0.0 copy-start
  0.0 1.4 %broadcast_in_dim.20 = bf16[16,8,576]{2,1,0:T(8,128)(2,1)} broadcast(bf16[8,576]{1,0:T(8,128)(2,1)} %param.10), dimensions={1,2} | broadcast | bytes 156672 | tf_op jit(solution)/shard_map/broadcast_in_dim | solution.py:265
  1.4 8.3 %all-to-all-start.8 = ((bf16[16,8,576]{2,1,0:T(8,128)(2,1)}), bf16[16,8,576]{2,1,0:T(8,128)(2,1)S(1)}, u32[]{:S(2)}, u32[]{:S(2)}) async-start(bf16[16,8,576]{2,1,0:T(8,128)(2,1)} %broadcast_in_dim.20), calls=%async_computation.8 | async-start | bytes 327680 | tf_op jit(solution)/shard_map/all_to_all | solution.py:265
  9.7 0.0 copy-done
  9.7 0.7 dynamic-slice_reduce_fusion.vert
  10.4 1.4 %dynamic-slice_reduce_fusion.1.slash = s32[4]{0:T(128)} fusion(s32[64,4]{0,1:T(4,128)} %param.12, s32[]{:T(128)S(6)} %select_n.4), kind=kLoop, calls=%fused_computation.1 | loop fusion | bytes 36 | tf_op jit(solution)/shard_map/dynamic_slice | solution.py:266
  11.8 0.1 pad_add_fusion.place
  11.9 2.3 %choice.1 = s32[8,32]{1,0:T(8,128)S(1)} custom-call(s32[2]{0:T(128)S(1)} %pad_add_fusion.place, s32[6]{0:T(128)} %dynamic-slice_reduce_fusion.vert, s32[4]{0:T(128)} %dynamic-slice_reduce_fusion.1.slash), custom_call_target="tpu_custom_call" | custom-call | tf_op jit(solution)/shard_map/choice/pallas_call | solution.py:51
  14.2 8.0 %all-to-all-done.8 = bf16[16,8,576]{2,1,0:T(8,128)(2,1)S(1)} async-done(((bf16[16,8,576]{2,1,0:T(8,128)(2,1)}), bf16[16,8,576]{2,1,0:T(8,128)(2,1)S(1)}, u32[]{:S(2)}, u32[]{:S(2)}) %all-to-all-start.8) | async-done | bytes 147488 | tf_op jit(solution)/shard_map/all_to_all | solution.py:265
  22.1 52.7 %conditional.1 = (bf16[2,512,128]{2,1,0:T(8,128)(2,1)S(1)}) conditional(s32[]{:T(128)} %clamp.3, (bf16[16,8,576]{2,1,0:T(8,128)(2,1)S(1)}, s32[2]{0:T(128)S(1)}, s32[8,32]{1,0:T(8,128)S(1)}, bf16[2,576,512]{2,1,0:T(8,128)(2,1)}, bf16[2,512,128]{2,1,0:T(8,128)(2,1)}) %tuple.26, (bf16[16,8,576]{2,1,0:T(8,128)(2,1)S(1)}, ...), branch_computations={%region_0.0_spmd, %region_1.0_spmd, %region_2.0_spmd, %region_3.0_... | conditional | flops 4294967296 | bytes 32440424 | solution.py:276
  22.1 0.9 %packed.7 = bf16[4,4,144,128]{3,2,1,0:T(8,128)(2,1)} custom-call(bf16[16,8,576]{2,1,0:T(8,128)(2,1)S(1)} %get-tuple-element.79.column_ref), custom_call_target="tpu_custom_call" | custom-call | tf_op jit(solution)/shard_map/cond/branch_3_fun/packed/pallas_call | solution.py:192
  23.0 11.5 %all_to_all.43 = bf16[4,4,144,128]{3,2,1,0:T(8,128)(2,1)S(1)} all-to-all(bf16[4,4,144,128]{3,2,1,0:T(8,128)(2,1)} %packed.7), channel_id=1, replica_groups={{0,4,8,12},{1,5,9,13},{2,6,10,14},{3,7,11,15},{16,20,24,28},{17,21,25,2..., dimensions={0} | all-to-all | bytes 1179648 | tf_op jit(solution)/shard_map/cond/branch_3_fun/all_to_all | solution.py:255
  34.5 0.4 broadcast_in_dim.14
  35.0 0.0 copy-start.4
  35.0 20.9 %all_to_all.44 = bf16[4,4,4,144,128]{4,3,2,1,0:T(8,128)(2,1)S(1)} all-to-all(bf16[4,4,4,144,128]{4,3,2,1,0:T(8,128)(2,1)S(1)} %broadcast_in_dim.14), channel_id=1, replica_groups={{0,16,32,48},{1,17,33,49},{2,18,34,50},{3,19,35,51},{4,20,36,52},{5,21,..., dimensions={0} | all-to-all | bytes 4718592 | tf_op jit(solution)/shard_map/cond/branch_3_fun/all_to_all | solution.py:255
  55.9 8.9 %collective-permute-start.3 = (bf16[16,4,144,128]{3,2,1,0:T(8,128)(2,1)S(1)}, bf16[16,4,144,128]{3,2,1,0:T(8,128)(2,1)S(1)}, u32[]{:S(2)}, u32[]{:S(2)}) collective-permute-start(bf16[16,4,144,128]{3,2,1,0:T(8,128)(2,1)S(1)} %bitcast.8), channel_id=1, source_target_pairs={{0,64},{1,65},{2,66},{3,67},{4,68},{5,69},{6,70},{7,71},{8,72},{9,... | collective-permute-start | bytes 7077896 | tf_op jit(solution)/shard_map/cond/branch_3_fun/ppermute | solution.py:272
  64.8 0.0 copy-done.4
  64.8 0.0 copy-start.8
  64.8 4.4 %own_half.7 = (bf16[4,256,640]{2,1,0:T(8,128)(2,1)S(1)}, f32[4,256,512]{2,1,0:T(8,128)S(1)}, f32[4,256,128]{2,1,0:T(8,128)S(1)}, f32[4,256,128]{2,1,0:T(8,128)S(1)}) custom-call(s32[2]{0:T(128)S(1)} %get-tuple-element.77.place, s32[8,32]{1,0:T(8,128)S(1)} %get-tuple-element.78.plan, bf16[2,576,512]{2,1,0:T(8,128)(2,1)S(1)} %copy-done.4, ...), custom_call_target="tpu_custom_call" | custom-call | flops 2147483648 | bytes 4194304 | tf_op jit(solution)/shard_map/cond/branch_3_fun/own_half/pallas_call | solution.py:208
  69.3 0.0 collective-permute-done.3.kv_ref
  69.3 0.0 copy-done.8
  69.3 5.2 %other_half.7 = bf16[2,512,128]{2,1,0:T(8,128)(2,1)S(1)} custom-call(s32[2]{0:T(128)S(1)} %get-tuple-element.77.place, s32[8,32]{1,0:T(8,128)S(1)} %get-tuple-element.78.plan, bf16[16,4,144,128]{3,2,1,0:T(8,128)(2,1)S(1)} %collective-permute-done.3.kv_ref, bf16[4,256,640]{2,1,0:T(8,128)(2,1)S(1)} %get-tuple-element.81.q_ref, ...), custom_call_target="tpu_custom_call" | custom-call | flops 2147483648 | bytes 4194304 | tf_op jit(solution)/shard_map/cond/branch_3_fun/other_half/pallas_call | solution.py:223
  74.8 0.0 copy-start.9
  74.8 0.7 copy-done.9
Async XLA Ops:
  0.0 9.7 %copy-start = (s32[64,6]{0,1:T(8,128)S(1)}, s32[64,6]{0,1:T(8,128)}, u32[]{:S(2)}) copy-start(s32[64,6]{0,1:T(8,128)} %param.11) | copy-start | bytes 4612
  1.4 20.7 %all-to-all-start.8 = ((bf16[16,8,576]{2,1,0:T(8,128)(2,1)}), bf16[16,8,576]{2,1,0:T(8,128)(2,1)S(1)}, u32[]{:S(2)}, u32[]{:S(2)}) async-start(bf16[16,8,576]{2,1,0:T(8,128)(2,1)} %broadcast_in_dim.20), calls=%async_computation.8 | async-start | bytes 327680 | tf_op jit(solution)/shard_map/all_to_all | solution.py:265
  35.0 29.8 %copy-start.4 = (bf16[2,576,512]{2,1,0:T(8,128)(2,1)S(1)}, bf16[2,576,512]{2,1,0:T(8,128)(2,1)}, u32[]{:S(2)}) copy-start(bf16[2,576,512]{2,1,0:T(8,128)(2,1)} %get-tuple-element.80.turned_ref) | copy-start | bytes 3538948 | tf_op jit(solution)/shard_map/cond
  55.9 13.4 %collective-permute-start.3 = (bf16[16,4,144,128]{3,2,1,0:T(8,128)(2,1)S(1)}, bf16[16,4,144,128]{3,2,1,0:T(8,128)(2,1)S(1)}, u32[]{:S(2)}, u32[]{:S(2)}) collective-permute-start(bf16[16,4,144,128]{3,2,1,0:T(8,128)(2,1)S(1)} %bitcast.8), channel_id=1, source_target_pairs={{0,64},{1,65},{2,66},{3,67},{4,68},{5,69},{6,70},{7,71},{8,72},{9,... | collective-permute-start | bytes 7077896 | tf_op jit(solution)/shard_map/cond/branch_3_fun/ppermute | solution.py:272
  64.8 4.5 %copy-start.8 = (bf16[2,512,128]{2,1,0:T(8,128)(2,1)S(1)}, bf16[2,512,128]{2,1,0:T(8,128)(2,1)}, u32[]{:S(2)}) copy-start(bf16[2,512,128]{2,1,0:T(8,128)(2,1)} %get-tuple-element.94.w_ref) | copy-start | bytes 786436 | tf_op jit(solution)/shard_map/cond
  74.8 0.7 copy-start.9

commit v5 on v4

--- a/solution.py
+++ b/solution.py
@@ -67,11 +67,11 @@
         start, step = jnp.where(half == 0, 4 * y, y), jnp.where(half == 0, 1, 4)
         for m in range(4):
             at = start + step * m
-            parts = [kv_ref[at, zh, 32 * t : 32 * t + 32, :] for t in range(4)]
-            if rotary:
-                both = kv_ref[at, zh, 128:, :]
-                parts.append(jnp.concatenate([both * side for side in sides], axis=0))
-            pieces.append(jnp.concatenate(parts, axis=1))
+            for side in range(2):
+                parts = [kv_ref[at, zh, 64 * side + 16 * t : 64 * side + 16 * t + 16, :] for t in range(4)]
+                if rotary:
+                    parts.append(kv_ref[at, zh, 128:, :] * sides[side])
+                pieces.append(jnp.concatenate(parts, axis=1))
     return jnp.concatenate(pieces, axis=0)
 
 
@@ -83,7 +83,9 @@
     left, right = s[:, :TILE], s[:, TILE:]
     if own_tile:
         at = lax.broadcasted_iota(jnp.int32, (HEADS * TILE, TILE), 0) & (TILE - 1)
-        left = jnp.where(lax.broadcasted_iota(jnp.int32, (HEADS * TILE, TILE), 1) <= at, left, DEAD)
+        col = lax.broadcasted_iota(jnp.int32, (HEADS * TILE, TILE), 1)
+        col = (col & 99) | ((col & 12) << 1) | ((col & 16) >> 2)
+        left = jnp.where(col <= at, left, DEAD)
     else:
         left = left + jnp.where(2 * p < plan[row, 31], 0.0, DEAD)
     right = right + jnp.where(2 * p + 1 < plan[row, 31], 0.0, DEAD)
@@ -178,12 +180,28 @@
 vmem = pl.BlockSpec(memory_space=pltpu.VMEM)
 
 
+def lay_beside(rows_ref, out_ref):
+    rows = rows_ref[...].astype(jnp.float32)
+    low, high = rows[:4], rows[4:]
+    block = jnp.concatenate([low[:, :LAT], high[:, :LAT], low[:, LAT:], high[:, LAT:]], axis=1).astype(jnp.bfloat16)
+    for n in range(16):
+        out_ref[n] = block
+
+
+def beside(rows):
+    return pl.pallas_call(
+        lay_beside,
+        out_shape=jax.ShapeDtypeStruct((16, 4, 2 * KV), jnp.bfloat16),
+        in_specs=[vmem],
+        out_specs=vmem,
+        name="beside",
+    )(rows)
+
+
 def pack(depth, column_ref, block_ref):
     for zh in range(depth):
         rows = jnp.concatenate([column_ref[4 * zh + n].astype(jnp.float32) for n in range(4)], axis=0)
-        rotary = jnp.concatenate([rows[:16, LAT:], rows[16:, LAT:]], axis=1)
-        block = jnp.concatenate([rows[:, n * TILE : (n + 1) * TILE] for n in range(4)] + [rotary], axis=0)
-        block = block.astype(jnp.bfloat16)
+        block = jnp.concatenate([rows[:, n * TILE : (n + 1) * TILE] for n in range(9)], axis=0).astype(jnp.bfloat16)
         for to in range(4):
             block_ref[to, zh] = block
 
@@ -262,7 +280,7 @@
     zh, core = lax.axis_index("zh"), lax.axis_index("core")
     grp_at = (lax.axis_index("y") * 4 + lax.axis_index("x")) * 4 + lax.axis_index("zl")
     place = jnp.stack([zh * 2 + core, core]).astype(jnp.int32)
-    column = lax.all_to_all(jnp.broadcast_to(kv_latent[None], (16, 8, KV)), ("zh", "zl"), 0, 0)
+    column = lax.all_to_all(beside(kv_latent), ("zh", "zl"), 0, 0)
     plan = choice(place, vert_tiles[grp_at], slash_offsets[grp_at])
     turned = queries.transpose(0, 2, 1)
 

time: 75.9 us -> 75.2 us (level)
  Pallas kernels: 12.8 us -> 14.2 us
  local copies, waits for them, and re-layouts: 4.64 us -> 3.25 us
    pallas_call x0 -> x1, Pallas kernels: none -> 1.45 us  [beside(): pl.pallas_call(lay_beside, out_shape=jax.ShapeDtypeStruct((16, 4, 2 * KV)...]
    broadcast_in_dim x1 -> x0, local copies, waits for them, and re-layouts: 1.39 us -> none  [on_device(): jnp.broadcast_to(kv_latent[None], (16, 8, KV))]
where the time goes in v5:
time: 75.2 us; the launch traced here: 74.8 us
  blocking collectives  32.3 us (43%)
  starting transfers between devices  17.2 us (23%)
  Pallas kernels  14.2 us (19%)
  waiting for transfers between devices  7.34 us (10%)
  local copies, waits for them, and re-layouts  3.25 us (4%)
    all_to_all x2, blocking collectives, to_all(): return lax.all_to_all(blocks, ALL, 0, 0, axis_index_groups=groups)  32.3 us
    ppermute x1, starting transfers between devices, plane(): other = lax.ppermute(own, ALL, other_core)  8.87 us
    all_to_all x1, starting transfers between devices, on_device(): column = lax.all_to_all(beside(kv_latent), ('zh', 'zl'), 0, 0)  8.29 us
    all_to_all x1, waiting for transfers between devices, on_device(): column = lax.all_to_all(beside(kv_latent), ('zh', 'zl'), 0, 0)  7.34 us
    pallas_call x1, Pallas kernels, other_half(): pl.pallas_call(functools.partial(attend_other, pairs, most > pairs), out_...  5.16 us
    pallas_call x1, Pallas kernels, own_half(): pl.pallas_call(functools.partial(attend_own, pairs, most > pairs), out_sh...  4.45 us
    pallas_call x1, Pallas kernels, choice(): pl.pallas_call(choose, out_shape=jax.ShapeDtypeStruct((2 * BLOCKS, 32), j...  2.3 us
    dynamic_slice x2, local copies, waits for them, and re-layouts, on_device(): plan = choice(place, vert_tiles[grp_at], slash_offsets[grp_at])  2.09 us
  transfers between devices with their start and end apart: 2, of which 1 were waited for; matrix products, arithmetic and copies ran while one was open for 3% of the time, Pallas kernels for 9%

profile of v5, /device:TPU:481, one launch (start us, length us, event | category | flops | bytes accessed | tf_op | source)
XLA Modules:
  0.0 74.8 jit_solution(17139667154316818553)
XLA Ops:
  0.0 0.0 copy-start
  0.0 1.5 %beside.1 = bf16[16,4,1152]{2,1,0:T(4,128)(2,1)} custom-call(bf16[8,576]{1,0:T(8,128)(2,1)} %rows_ref.1), custom_call_target="tpu_custom_call" | custom-call | tf_op jit(solution)/shard_map/beside/pallas_call | solution.py:192
  1.5 8.3 %all-to-all-start.8 = ((bf16[16,4,1152]{2,1,0:T(4,128)(2,1)}), bf16[16,4,1152]{2,1,0:T(4,128)(2,1)S(1)}, u32[]{:S(2)}, u32[]{:S(2)}) async-start(bf16[16,4,1152]{2,1,0:T(4,128)(2,1)} %beside.1), calls=%async_computation.8 | async-start | bytes 294912 | tf_op jit(solution)/shard_map/all_to_all | solution.py:283
  9.8 0.0 copy-done
  9.8 0.7 dynamic-slice_reduce_fusion.vert
  10.5 1.4 %dynamic-slice_reduce_fusion.1.slash = s32[4]{0:T(128)} fusion(s32[64,4]{0,1:T(4,128)} %param.12, s32[]{:T(128)S(6)} %select_n.4), kind=kLoop, calls=%fused_computation.1 | loop fusion | bytes 36 | tf_op jit(solution)/shard_map/dynamic_slice | solution.py:284
  11.8 0.1 pad_add_fusion.place
  11.9 2.3 %choice.1 = s32[8,32]{1,0:T(8,128)S(1)} custom-call(s32[2]{0:T(128)S(1)} %pad_add_fusion.place, s32[6]{0:T(128)} %dynamic-slice_reduce_fusion.vert, s32[4]{0:T(128)} %dynamic-slice_reduce_fusion.1.slash), custom_call_target="tpu_custom_call" | custom-call | tf_op jit(solution)/shard_map/choice/pallas_call | solution.py:51
  14.2 7.3 %all-to-all-done.8 = bf16[16,4,1152]{2,1,0:T(4,128)(2,1)S(1)} async-done(((bf16[16,4,1152]{2,1,0:T(4,128)(2,1)}), bf16[16,4,1152]{2,1,0:T(4,128)(2,1)S(1)}, u32[]{:S(2)}, u32[]{:S(2)}) %all-to-all-start.8) | async-done | bytes 147488 | tf_op jit(solution)/shard_map/all_to_all | solution.py:283
  21.6 52.5 %conditional.1 = (bf16[2,512,128]{2,1,0:T(8,128)(2,1)S(1)}) conditional(s32[]{:T(128)} %clamp.3, (bf16[16,4,1152]{2,1,0:T(4,128)(2,1)S(1)}, s32[2]{0:T(128)S(1)}, s32[8,32]{1,0:T(8,128)S(1)}, bf16[2,576,512]{2,1,0:T(8,128)(2,1)}, bf16[2,512,128]{2,1,0:T(8,128)(2,1)}) %tuple.26, (bf16[16,4,1152]{2,1,0:T(4,128)(2,1)S(1)}, ...), branch_computations={%region_0.0_spmd, %region_1.0_spmd, %region_2.0_spmd, %region_3.0_... | conditional | flops 4294967296 | bytes 32440424 | solution.py:294
  21.6 0.9 %packed.7 = bf16[4,4,144,128]{3,2,1,0:T(8,128)(2,1)} custom-call(bf16[16,4,1152]{2,1,0:T(4,128)(2,1)S(1)} %get-tuple-element.79.column_ref), custom_call_target="tpu_custom_call" | custom-call | tf_op jit(solution)/shard_map/cond/branch_3_fun/packed/pallas_call | solution.py:210
  22.4 11.5 %all_to_all.43 = bf16[4,4,144,128]{3,2,1,0:T(8,128)(2,1)S(1)} all-to-all(bf16[4,4,144,128]{3,2,1,0:T(8,128)(2,1)} %packed.7), channel_id=1, replica_groups={{0,4,8,12},{1,5,9,13},{2,6,10,14},{3,7,11,15},{16,20,24,28},{17,21,25,2..., dimensions={0} | all-to-all | bytes 1179648 | tf_op jit(solution)/shard_map/cond/branch_3_fun/all_to_all | solution.py:273
  33.9 0.4 broadcast_in_dim.17
  34.4 0.0 copy-start.4
  34.4 20.9 %all_to_all.44 = bf16[4,4,4,144,128]{4,3,2,1,0:T(8,128)(2,1)S(1)} all-to-all(bf16[4,4,4,144,128]{4,3,2,1,0:T(8,128)(2,1)S(1)} %broadcast_in_dim.17), channel_id=1, replica_groups={{0,16,32,48},{1,17,33,49},{2,18,34,50},{3,19,35,51},{4,20,36,52},{5,21,..., dimensions={0} | all-to-all | bytes 4718592 | tf_op jit(solution)/shard_map/cond/branch_3_fun/all_to_all | solution.py:273
  55.3 8.9 %collective-permute-start.3 = (bf16[16,4,144,128]{3,2,1,0:T(8,128)(2,1)S(1)}, bf16[16,4,144,128]{3,2,1,0:T(8,128)(2,1)S(1)}, u32[]{:S(2)}, u32[]{:S(2)}) collective-permute-start(bf16[16,4,144,128]{3,2,1,0:T(8,128)(2,1)S(1)} %bitcast.8), channel_id=1, source_target_pairs={{0,64},{1,65},{2,66},{3,67},{4,68},{5,69},{6,70},{7,71},{8,72},{9,... | collective-permute-start | bytes 7077896 | tf_op jit(solution)/shard_map/cond/branch_3_fun/ppermute | solution.py:290
  64.1 0.0 copy-done.4
  64.1 0.0 copy-start.8
  64.2 4.5 %own_half.7 = (bf16[4,256,640]{2,1,0:T(8,128)(2,1)S(1)}, f32[4,256,512]{2,1,0:T(8,128)S(1)}, f32[4,256,128]{2,1,0:T(8,128)S(1)}, f32[4,256,128]{2,1,0:T(8,128)S(1)}) custom-call(s32[2]{0:T(128)S(1)} %get-tuple-element.77.place, s32[8,32]{1,0:T(8,128)S(1)} %get-tuple-element.78.plan, bf16[2,576,512]{2,1,0:T(8,128)(2,1)S(1)} %copy-done.4, ...), custom_call_target="tpu_custom_call" | custom-call | flops 2147483648 | bytes 4194304 | tf_op jit(solution)/shard_map/cond/branch_3_fun/own_half/pallas_call | solution.py:226
  68.6 0.0 collective-permute-done.3.kv_ref
  68.6 0.0 copy-done.8
  68.6 5.2 %other_half.7 = bf16[2,512,128]{2,1,0:T(8,128)(2,1)S(1)} custom-call(s32[2]{0:T(128)S(1)} %get-tuple-element.77.place, s32[8,32]{1,0:T(8,128)S(1)} %get-tuple-element.78.plan, bf16[16,4,144,128]{3,2,1,0:T(8,128)(2,1)S(1)} %collective-permute-done.3.kv_ref, bf16[4,256,640]{2,1,0:T(8,128)(2,1)S(1)} %get-tuple-element.81.q_ref, ...), custom_call_target="tpu_custom_call" | custom-call | flops 2147483648 | bytes 4194304 | tf_op jit(solution)/shard_map/cond/branch_3_fun/other_half/pallas_call | solution.py:241
  74.1 0.0 copy-start.9
  74.1 0.7 copy-done.9
Async XLA Ops:
  0.0 9.8 %copy-start = (s32[64,6]{0,1:T(8,128)S(1)}, s32[64,6]{0,1:T(8,128)}, u32[]{:S(2)}) copy-start(s32[64,6]{0,1:T(8,128)} %param.11) | copy-start | bytes 4612
  1.5 20.1 %all-to-all-start.8 = ((bf16[16,4,1152]{2,1,0:T(4,128)(2,1)}), bf16[16,4,1152]{2,1,0:T(4,128)(2,1)S(1)}, u32[]{:S(2)}, u32[]{:S(2)}) async-start(bf16[16,4,1152]{2,1,0:T(4,128)(2,1)} %beside.1), calls=%async_computation.8 | async-start | bytes 294912 | tf_op jit(solution)/shard_map/all_to_all | solution.py:283
  34.4 29.8 %copy-start.4 = (bf16[2,576,512]{2,1,0:T(8,128)(2,1)S(1)}, bf16[2,576,512]{2,1,0:T(8,128)(2,1)}, u32[]{:S(2)}) copy-start(bf16[2,576,512]{2,1,0:T(8,128)(2,1)} %get-tuple-element.80.turned_ref) | copy-start | bytes 3538948 | tf_op jit(solution)/shard_map/cond
  55.3 13.4 %collective-permute-start.3 = (bf16[16,4,144,128]{3,2,1,0:T(8,128)(2,1)S(1)}, bf16[16,4,144,128]{3,2,1,0:T(8,128)(2,1)S(1)}, u32[]{:S(2)}, u32[]{:S(2)}) collective-permute-start(bf16[16,4,144,128]{3,2,1,0:T(8,128)(2,1)S(1)} %bitcast.8), channel_id=1, source_target_pairs={{0,64},{1,65},{2,66},{3,67},{4,68},{5,69},{6,70},{7,71},{8,72},{9,... | collective-permute-start | bytes 7077896 | tf_op jit(solution)/shard_map/cond/branch_3_fun/ppermute | solution.py:290
  64.1 4.5 %copy-start.8 = (bf16[2,512,128]{2,1,0:T(8,128)(2,1)S(1)}, bf16[2,512,128]{2,1,0:T(8,128)(2,1)}, u32[]{:S(2)}) copy-start(bf16[2,512,128]{2,1,0:T(8,128)(2,1)} %get-tuple-element.94.w_ref) | copy-start | bytes 786436 | tf_op jit(solution)/shard_map/cond
  74.1 0.7 copy-start.9

commit v6 on v5

--- a/solution.py
+++ b/solution.py
@@ -158,7 +158,7 @@
         rest(pairs, plan, 0, place[1], kv_ref, q_ref, acc_ref, top_ref, total_ref)
 
 
-def attend_other(pairs, more, place, plan, kv_ref, q_ref, acc_in, top_in, total_in, w_ref, out_ref, s_ref, latent_ref, *state):
+def attend_other(pairs, more, place, plan, kv_ref, q_ref, acc_in, top_in, total_in, w_ref, out_ref, s_ref, *state):
     half = 1 - place[1]
     if more:
         for held, given in zip(state, (acc_in, top_in, total_in)):
@@ -169,11 +169,10 @@
         top, total, acc = many(
             q_ref[b], pairs, False, plan, BLOCKS + b, half, kv_ref, s_ref.at[b % 2], top_ref[b], total_ref[b], acc_ref[b]
         )
-        latent_ref[b] = (acc * wide(1.0 / total, LAT // TILE)).astype(jnp.bfloat16)
-    for h in range(HEADS):
-        latent = jnp.concatenate([latent_ref[b, h * TILE : (h + 1) * TILE] for b in range(BLOCKS)], axis=0)
-        up = jnp.dot(latent, w_ref[h], preferred_element_type=jnp.float32)
-        out_ref[h] = up.astype(jnp.bfloat16)
+        latent = (acc * wide(1.0 / total, LAT // TILE)).astype(jnp.bfloat16)
+        for h in range(HEADS):
+            up = jnp.dot(latent[h * TILE : (h + 1) * TILE], w_ref[h], preferred_element_type=jnp.float32)
+            out_ref[h, b * TILE : (b + 1) * TILE, :] = up.astype(jnp.bfloat16)
 
 
 smem = pl.BlockSpec(memory_space=pltpu.SMEM)
@@ -245,7 +244,6 @@
         out_specs=vmem,
         scratch_shapes=[
             pltpu.VMEM((2, HEADS * TILE, 2 * pairs * TILE), jnp.float32),
-            pltpu.VMEM((BLOCKS, HEADS * TILE, LAT), jnp.bfloat16),
             *(pltpu.VMEM(a.shape, a.dtype) for a in accumulated if most > pairs),
         ],
         compiler_params=pltpu.CompilerParams(vmem_limit_bytes=16 * 1024 * 1024),

time: 75.2 us -> 75.6 us (level)
  no operation moved by 1% of the time
where the time goes in v6:
time: 75.6 us; the launch traced here: 75.2 us
  blocking collectives  32.3 us (43%)
  starting transfers between devices  17.2 us (23%)
  Pallas kernels  14.6 us (19%)
  waiting for transfers between devices  7.34 us (10%)
  local copies, waits for them, and re-layouts  3.25 us (4%)
    all_to_all x2, blocking collectives, to_all(): return lax.all_to_all(blocks, ALL, 0, 0, axis_index_groups=groups)  32.3 us
    ppermute x1, starting transfers between devices, plane(): other = lax.ppermute(own, ALL, other_core)  8.87 us
    all_to_all x1, starting transfers between devices, on_device(): column = lax.all_to_all(beside(kv_latent), ('zh', 'zl'), 0, 0)  8.29 us
    all_to_all x1, waiting for transfers between devices, on_device(): column = lax.all_to_all(beside(kv_latent), ('zh', 'zl'), 0, 0)  7.34 us
    pallas_call x1, Pallas kernels, other_half(): pl.pallas_call(functools.partial(attend_other, pairs, most > pairs), out_...  5.54 us
    pallas_call x1, Pallas kernels, own_half(): pl.pallas_call(functools.partial(attend_own, pairs, most > pairs), out_sh...  4.47 us
    pallas_call x1, Pallas kernels, choice(): pl.pallas_call(choose, out_shape=jax.ShapeDtypeStruct((2 * BLOCKS, 32), j...  2.3 us
    dynamic_slice x2, local copies, waits for them, and re-layouts, on_device(): plan = choice(place, vert_tiles[grp_at], slash_offsets[grp_at])  2.09 us
  transfers between devices with their start and end apart: 2, of which 1 were waited for; matrix products, arithmetic and copies ran while one was open for 3% of the time, Pallas kernels for 9%

profile of v6, /device:TPU:481, one launch (start us, length us, event | category | flops | bytes accessed | tf_op | source)
XLA Modules:
  0.0 75.2 jit_solution(7249947826500813153)
XLA Ops:
  0.0 0.0 copy-start
  0.0 1.5 %beside.1 = bf16[16,4,1152]{2,1,0:T(4,128)(2,1)} custom-call(bf16[8,576]{1,0:T(8,128)(2,1)} %rows_ref.1), custom_call_target="tpu_custom_call" | custom-call | tf_op jit(solution)/shard_map/beside/pallas_call | solution.py:191
  1.5 8.3 %all-to-all-start.8 = ((bf16[16,4,1152]{2,1,0:T(4,128)(2,1)}), bf16[16,4,1152]{2,1,0:T(4,128)(2,1)S(1)}, u32[]{:S(2)}, u32[]{:S(2)}) async-start(bf16[16,4,1152]{2,1,0:T(4,128)(2,1)} %beside.1), calls=%async_computation.8 | async-start | bytes 294912 | tf_op jit(solution)/shard_map/all_to_all | solution.py:281
  9.8 0.0 copy-done
  9.8 0.7 dynamic-slice_reduce_fusion.vert
  10.5 1.4 %dynamic-slice_reduce_fusion.1.slash = s32[4]{0:T(128)} fusion(s32[64,4]{0,1:T(4,128)} %param.12, s32[]{:T(128)S(6)} %select_n.4), kind=kLoop, calls=%fused_computation.1 | loop fusion | bytes 36 | tf_op jit(solution)/shard_map/dynamic_slice | solution.py:282
  11.8 0.1 pad_add_fusion.place
  11.9 2.3 %choice.1 = s32[8,32]{1,0:T(8,128)S(1)} custom-call(s32[2]{0:T(128)S(1)} %pad_add_fusion.place, s32[6]{0:T(128)} %dynamic-slice_reduce_fusion.vert, s32[4]{0:T(128)} %dynamic-slice_reduce_fusion.1.slash), custom_call_target="tpu_custom_call" | custom-call | tf_op jit(solution)/shard_map/choice/pallas_call | solution.py:51
  14.2 7.3 %all-to-all-done.8 = bf16[16,4,1152]{2,1,0:T(4,128)(2,1)S(1)} async-done(((bf16[16,4,1152]{2,1,0:T(4,128)(2,1)}), bf16[16,4,1152]{2,1,0:T(4,128)(2,1)S(1)}, u32[]{:S(2)}, u32[]{:S(2)}) %all-to-all-start.8) | async-done | bytes 147488 | tf_op jit(solution)/shard_map/all_to_all | solution.py:281
  21.6 52.9 %conditional.1 = (bf16[2,512,128]{2,1,0:T(8,128)(2,1)S(1)}) conditional(s32[]{:T(128)} %clamp.3, (bf16[16,4,1152]{2,1,0:T(4,128)(2,1)S(1)}, s32[2]{0:T(128)S(1)}, s32[8,32]{1,0:T(8,128)S(1)}, bf16[2,576,512]{2,1,0:T(8,128)(2,1)}, bf16[2,512,128]{2,1,0:T(8,128)(2,1)}) %tuple.26, (bf16[16,4,1152]{2,1,0:T(4,128)(2,1)S(1)}, ...), branch_computations={%region_0.0_spmd, %region_1.0_spmd, %region_2.0_spmd, %region_3.0_... | conditional | flops 4294967296 | bytes 32440424 | solution.py:292
  21.6 0.9 %packed.7 = bf16[4,4,144,128]{3,2,1,0:T(8,128)(2,1)} custom-call(bf16[16,4,1152]{2,1,0:T(4,128)(2,1)S(1)} %get-tuple-element.79.column_ref), custom_call_target="tpu_custom_call" | custom-call | tf_op jit(solution)/shard_map/cond/branch_3_fun/packed/pallas_call | solution.py:209
  22.4 11.5 %all_to_all.43 = bf16[4,4,144,128]{3,2,1,0:T(8,128)(2,1)S(1)} all-to-all(bf16[4,4,144,128]{3,2,1,0:T(8,128)(2,1)} %packed.7), channel_id=1, replica_groups={{0,4,8,12},{1,5,9,13},{2,6,10,14},{3,7,11,15},{16,20,24,28},{17,21,25,2..., dimensions={0} | all-to-all | bytes 1179648 | tf_op jit(solution)/shard_map/cond/branch_3_fun/all_to_all | solution.py:271
  33.9 0.4 broadcast_in_dim.17
  34.4 0.0 copy-start.4
  34.4 20.9 %all_to_all.44 = bf16[4,4,4,144,128]{4,3,2,1,0:T(8,128)(2,1)S(1)} all-to-all(bf16[4,4,4,144,128]{4,3,2,1,0:T(8,128)(2,1)S(1)} %broadcast_in_dim.17), channel_id=1, replica_groups={{0,16,32,48},{1,17,33,49},{2,18,34,50},{3,19,35,51},{4,20,36,52},{5,21,..., dimensions={0} | all-to-all | bytes 4718592 | tf_op jit(solution)/shard_map/cond/branch_3_fun/all_to_all | solution.py:271
  55.3 8.9 %collective-permute-start.3 = (bf16[16,4,144,128]{3,2,1,0:T(8,128)(2,1)S(1)}, bf16[16,4,144,128]{3,2,1,0:T(8,128)(2,1)S(1)}, u32[]{:S(2)}, u32[]{:S(2)}) collective-permute-start(bf16[16,4,144,128]{3,2,1,0:T(8,128)(2,1)S(1)} %bitcast.8), channel_id=1, source_target_pairs={{0,64},{1,65},{2,66},{3,67},{4,68},{5,69},{6,70},{7,71},{8,72},{9,... | collective-permute-start | bytes 7077896 | tf_op jit(solution)/shard_map/cond/branch_3_fun/ppermute | solution.py:288
  64.1 0.0 copy-done.4
  64.1 0.0 copy-start.8
  64.2 4.5 %own_half.7 = (bf16[4,256,640]{2,1,0:T(8,128)(2,1)S(1)}, f32[4,256,512]{2,1,0:T(8,128)S(1)}, f32[4,256,128]{2,1,0:T(8,128)S(1)}, f32[4,256,128]{2,1,0:T(8,128)S(1)}) custom-call(s32[2]{0:T(128)S(1)} %get-tuple-element.77.place, s32[8,32]{1,0:T(8,128)S(1)} %get-tuple-element.78.plan, bf16[2,576,512]{2,1,0:T(8,128)(2,1)S(1)} %copy-done.4, ...), custom_call_target="tpu_custom_call" | custom-call | flops 2147483648 | bytes 4194304 | tf_op jit(solution)/shard_map/cond/branch_3_fun/own_half/pallas_call | solution.py:225
  68.6 0.0 collective-permute-done.3.kv_ref
  68.6 0.0 copy-done.8
  68.7 5.5 %other_half.7 = bf16[2,512,128]{2,1,0:T(8,128)(2,1)S(1)} custom-call(s32[2]{0:T(128)S(1)} %get-tuple-element.77.place, s32[8,32]{1,0:T(8,128)S(1)} %get-tuple-element.78.plan, bf16[16,4,144,128]{3,2,1,0:T(8,128)(2,1)S(1)} %collective-permute-done.3.kv_ref, bf16[4,256,640]{2,1,0:T(8,128)(2,1)S(1)} %get-tuple-element.81.q_ref, ...), custom_call_target="tpu_custom_call" | custom-call | flops 2147483648 | bytes 4194304 | tf_op jit(solution)/shard_map/cond/branch_3_fun/other_half/pallas_call | solution.py:240
  74.5 0.0 copy-start.9
  74.5 0.7 copy-done.9
Async XLA Ops:
  0.0 9.8 %copy-start = (s32[64,6]{0,1:T(8,128)S(1)}, s32[64,6]{0,1:T(8,128)}, u32[]{:S(2)}) copy-start(s32[64,6]{0,1:T(8,128)} %param.11) | copy-start | bytes 4612
  1.5 20.1 %all-to-all-start.8 = ((bf16[16,4,1152]{2,1,0:T(4,128)(2,1)}), bf16[16,4,1152]{2,1,0:T(4,128)(2,1)S(1)}, u32[]{:S(2)}, u32[]{:S(2)}) async-start(bf16[16,4,1152]{2,1,0:T(4,128)(2,1)} %beside.1), calls=%async_computation.8 | async-start | bytes 294912 | tf_op jit(solution)/shard_map/all_to_all | solution.py:281
  34.4 29.8 %copy-start.4 = (bf16[2,576,512]{2,1,0:T(8,128)(2,1)S(1)}, bf16[2,576,512]{2,1,0:T(8,128)(2,1)}, u32[]{:S(2)}) copy-start(bf16[2,576,512]{2,1,0:T(8,128)(2,1)} %get-tuple-element.80.turned_ref) | copy-start | bytes 3538948 | tf_op jit(solution)/shard_map/cond
  55.3 13.4 %collective-permute-start.3 = (bf16[16,4,144,128]{3,2,1,0:T(8,128)(2,1)S(1)}, bf16[16,4,144,128]{3,2,1,0:T(8,128)(2,1)S(1)}, u32[]{:S(2)}, u32[]{:S(2)}) collective-permute-start(bf16[16,4,144,128]{3,2,1,0:T(8,128)(2,1)S(1)} %bitcast.8), channel_id=1, source_target_pairs={{0,64},{1,65},{2,66},{3,67},{4,68},{5,69},{6,70},{7,71},{8,72},{9,... | collective-permute-start | bytes 7077896 | tf_op jit(solution)/shard_map/cond/branch_3_fun/ppermute | solution.py:288
  64.1 4.5 %copy-start.8 = (bf16[2,512,128]{2,1,0:T(8,128)(2,1)S(1)}, bf16[2,512,128]{2,1,0:T(8,128)(2,1)}, u32[]{:S(2)}) copy-start(bf16[2,512,128]{2,1,0:T(8,128)(2,1)} %get-tuple-element.94.w_ref) | copy-start | bytes 786436 | tf_op jit(solution)/shard_map/cond
  74.5 0.7 copy-start.9
